TPU v7x, 256 devices: a whole 4x4x8 slice. The times are simulated.
256 devices in a mesh: seq: 64 (over y, z, core), head: 4 (over x).
Axes of the slice: x: 4, y: 4, z: 8, core: 2. Of those that a mesh axis runs over, the one named last changes fastest.
Arguments:
- inputs: bfloat16 [32768, 4096], P('seq', 'head'), may hold values from -6 to 6
- rows_b: bfloat16 [32768, 128], P('seq'), may hold values from -6 to 6
- rows_c: bfloat16 [32768, 128], P('seq'), may hold values from -0.5 to 0.5
- log_decay: float32 [64, 32768], P('head', 'seq'), may hold values from -1 to 0, as said below
- score_cotangent: bfloat16 [32768, 2048], P('seq', 'head'), may hold values from -6 to 6
- out_weight: bfloat16 [4096, 2048], P('head'), may hold values from -0.09375 to 0.09375
Outputs:
- critic_hidden: bfloat16 [32768, 2048], P('seq', 'head')
- input_grad: bfloat16 [32768, 4096], P('seq', 'head')
- score_grad: bfloat16 [32768, 2048], P('seq', 'head')
Inputs may be any that keep to these rules, and one draw needn't show every extreme that they name: `log_decay`: every entry is below zero.
All inputs are finite; a program needn't handle non-finite values.
Results may differ from a plain program's by a relative error of at most 0.025.
Values may be sent and summed in bfloat16 or wider, within the bound.
A program may use at most 192 MiB of HBM per device.

v0:
```python
import jax
import jax.numpy as jnp
from jax import lax
from jax.sharding import PartitionSpec as P

Q = 256


highest = lax.Precision.HIGHEST


def shortened(shard):

    def short(part):
        return part.astype(jnp.bfloat16) if part.dtype == jnp.float32 else part

    return jax.tree.map(short, shard)


def decay_tables(log_rates):
    cumulative = jnp.cumsum(log_rates, axis=1)
    spread = cumulative[:, :, None] - cumulative[:, None, :]
    length = log_rates.shape[1]
    lower_mask = (jnp.arange(length)[:, None] >= jnp.arange(length)[None, :])[None]
    within = jnp.where(lower_mask, jnp.exp(jnp.where(lower_mask, spread, 0.0)), 0.0)
    weight = jnp.sqrt(-jnp.expm1(2.0 * log_rates))
    return (cumulative, within, weight)


def prepare(rows_b, rows_c, log_rates):
    cumulative, within, weight = decay_tables(log_rates)
    scores = jnp.dot(rows_c, rows_b.T, preferred_element_type=jnp.float32)
    return (
        cumulative,
        within,
        weight,
        scores,
        rows_b.astype(jnp.float32),
        rows_c.astype(jnp.float32),
    )


def state_read(rows_map, state):
    head_count, state_rows, head_width = state.shape
    flat_state = state.transpose(1, 0, 2).reshape(state_rows, head_count * head_width)
    product = jnp.dot(rows_map, flat_state, precision=highest, preferred_element_type=jnp.float32)
    return product.reshape(rows_map.shape[0], head_count, head_width)


def state_write(rows_map, driven):
    frames, head_count, head_width = driven.shape
    flat_driven = driven.reshape(frames, head_count * head_width)
    product = lax.dot_general(
        rows_map,
        flat_driven,
        (((0,), (0,)), ((), ())),
        precision=highest,
        preferred_element_type=jnp.float32,
    )
    return product.reshape(rows_map.shape[1], head_count, head_width).transpose(1, 0, 2)


def block_forward(values, prepared, carry_state):
    cumulative, within, weight, scores, b_float, c_float = prepared
    head_count = cumulative.shape[0]
    frames = values.shape[0]
    driven = values.astype(jnp.float32).reshape(frames, head_count, -1) * weight.T[:, :, None]
    mixing = within * scores[None]
    intra_part = jnp.einsum("hts,shp->thp", mixing, driven, precision=highest)
    carried = jnp.exp(cumulative).T[:, :, None] * state_read(c_float, carry_state)
    tail_decay = jnp.exp(cumulative[:, -1:] - cumulative)
    new_state = jnp.exp(cumulative[:, -1])[:, None, None] * carry_state + state_write(
        b_float, driven * tail_decay.T[:, :, None]
    )
    return ((intra_part + carried).reshape(frames, -1), new_state)


def block_reverse(values, prepared, carry_state):
    cumulative, within, weight, scores, b_float, c_float = prepared
    head_count = cumulative.shape[0]
    frames = values.shape[0]
    driven = values.astype(jnp.float32).reshape(frames, head_count, -1)
    mixing = within * scores[None]
    intra_part = jnp.einsum("hst,shp->thp", mixing, driven, precision=highest)
    tail_decay = jnp.exp(cumulative[:, -1:] - cumulative)
    carried = tail_decay.T[:, :, None] * state_read(b_float, carry_state)
    result = weight.T[:, :, None] * (intra_part + carried)
    new_state = jnp.exp(cumulative[:, -1])[:, None, None] * carry_state + state_write(
        c_float, driven * jnp.exp(cumulative).T[:, :, None]
    )
    return (result.reshape(frames, -1), new_state)


def carry_incoming(end_state, total_log, backwards):
    head_count = end_state.shape[0]
    flattened = end_state.reshape(head_count, -1)
    pieces = lax.all_to_all(
        flattened[None].astype(jnp.bfloat16), "seq", split_axis=2, concat_axis=0, tiled=True
    ).astype(jnp.float32)
    totals = lax.all_gather(total_log[None], "seq", axis=0, tiled=True)
    running = jnp.cumsum(totals, axis=0)
    before = running - totals
    seq_count = totals.shape[0]
    target = jnp.arange(seq_count)[:, None]
    source = jnp.arange(seq_count)[None, :]
    if backwards:
        exponent = before[None, :, :] - running[:, None, :]
        source_mask = (source > target)[:, :, None]
    else:
        exponent = before[:, None, :] - running[None, :, :]
        source_mask = (source < target)[:, :, None]
    weights = jnp.where(source_mask, jnp.exp(jnp.where(source_mask, exponent, 0.0)), 0.0)
    mixed_sum = jnp.einsum("deh,ehk->dhk", weights, pieces, precision=highest)
    returned = lax.all_to_all(
        shortened(mixed_sum), "seq", split_axis=0, concat_axis=2, tiled=True
    ).astype(mixed_sum.dtype)
    return returned.reshape(end_state.shape)


def head_project(rows, out_weight):
    partial_value = jnp.dot(rows, out_weight, preferred_element_type=jnp.float32)
    return lax.psum_scatter(
        partial_value.astype(jnp.bfloat16), "head", scatter_dimension=1, tiled=True
    )


def local(inputs, rows_b, rows_c, log_decay, score_cotangent, out_weight):
    frames = inputs.shape[0]
    head_count = log_decay.shape[0]
    state_rows = rows_b.shape[1]
    head_width = inputs.shape[1] // head_count
    block_count = frames // Q
    prepared = [
        prepare(
            rows_b[i * Q : (i + 1) * Q],
            rows_c[i * Q : (i + 1) * Q],
            log_decay[:, i * Q : (i + 1) * Q],
        )
        for i in range(block_count)
    ]
    dev_cumul = jnp.cumsum(log_decay, axis=1)
    total_log = dev_cumul[:, -1]
    weight_dev = jnp.sqrt(-jnp.expm1(2.0 * log_decay))
    rise = jnp.exp(dev_cumul).T[:, :, None]
    fall = (weight_dev * jnp.exp(total_log[:, None] - dev_cumul)).T[:, :, None]
    b_all = rows_b.astype(jnp.float32)
    c_all = rows_c.astype(jnp.float32)
    zero_state = jnp.zeros((head_count, state_rows, head_width), jnp.float32)

    def forward_op(values):
        carry_state = zero_state
        outputs = []
        for block_index in range(block_count):
            output, carry_state = block_forward(
                values[block_index * Q : (block_index + 1) * Q], prepared[block_index], carry_state
            )
            outputs.append(output)
        incoming = carry_incoming(carry_state, total_log, False)
        extra = rise * state_read(c_all, incoming)
        return jnp.concatenate(outputs, axis=0) + extra.reshape(frames, -1)

    mixed = forward_op(inputs).astype(jnp.bfloat16)
    critic_hidden = head_project(mixed, out_weight)
    pulled = jnp.dot(
        lax.all_gather(score_cotangent, "head", axis=1, tiled=True),
        out_weight.T,
        preferred_element_type=jnp.float32,
    ).astype(jnp.bfloat16)
    carry_state = zero_state
    outputs = []
    for block_index in range(block_count - 1, -1, -1):
        output, carry_state = block_reverse(
            pulled[block_index * Q : (block_index + 1) * Q], prepared[block_index], carry_state
        )
        outputs.append(output)
    ordered = outputs[::-1]
    incoming = carry_incoming(carry_state, total_log, True)
    extra = fall * state_read(b_all, incoming)
    input_grad = (jnp.concatenate(ordered, axis=0) + extra.reshape(frames, -1)).astype(jnp.bfloat16)
    tangent = (2.0 * forward_op(input_grad)).astype(jnp.bfloat16)
    score_grad = head_project(tangent, out_weight)
    return (critic_hidden, input_grad, score_grad)


def solution(mesh):
    return jax.shard_map(
        local,
        mesh=mesh,
        in_specs=(
            P("seq", "head"),
            P("seq", None),
            P("seq", None),
            P("head", "seq"),
            P("seq", "head"),
            P("head", None),
        ),
        out_specs=(P("seq", "head"), P("seq", "head"), P("seq", "head")),
        check_vma=False,
    )
```

profile of v0, /device:TPU:1, one launch (start us, length us, event | category | flops | bytes accessed | tf_op | source)
XLA Modules:
  0.0 576.8 jit_solution(14242754907038339348)
XLA Ops:
  7.9 1.4 sqrt_bitcast_fusion
  13.8 128.3 %all-reduce = f32[1024]{0:T(1024)S(1)} all-reduce(f32[1024]{0:T(1024)S(1)} %dynamic-update-slice), channel_id=2, replica_groups=mesh['seq'=64,'head'=4] {'seq'}, use_global_device_ids=true, to_apply=%add | all-reduce | flops 1024 | bytes 8192
  156.1 1.4 multiply_bitcast_fusion
  159.3 1.5 fusion.95
  160.8 1.6 fusion.97
  162.4 5.2 convolution_convert_fusion.2
  170.6 6.7 %copy.142 = bf16[1,16,8192]{1,0,2:T(2,128)(2,1)} copy(bf16[1,16,8192]{2,1,0:T(8,128)(2,1)S(1)} %convert_element_type.131) | data formatting | bytes 524288 | tf_op jit(solution)/shard_map/convert_element_type | solution.py:98
  177.8 45.4 %reduce.12 = bf16[8192,16]{1,0:T(8,128)(2,1)S(1)} reduce(bf16[8192,1,16]{2,1,0:T(2,128)(2,1)} %bitcast.282, bf16[]{:T(256)} %broadcast.114), dimensions={1}, to_apply=%bitcast.246.reduce_sub_computation | reduce | bytes 524290
  223.2 3.0 reshape.355
  226.2 9.1 %all-to-all-start.2 = ((bf16[64,2,1024]{2,1,0:T(2,128)(2,1)}), bf16[64,2,1024]{2,1,0:T(2,128)(2,1)S(1)}, u32[]{:S(2)}, u32[]{:S(2)}) async-start(bf16[64,2,1024]{2,1,0:T(2,128)(2,1)} %reshape.355), calls=%async_computation.3 | async-start | bytes 524288 | tf_op jit(solution)/shard_map/all_to_all | solution.py:97
  237.5 1.6 fusion.70
  239.2 8.1 %all-to-all-done.2 = bf16[64,2,1024]{2,1,0:T(2,128)(2,1)S(1)} async-done(((bf16[64,2,1024]{2,1,0:T(2,128)(2,1)}), bf16[64,2,1024]{2,1,0:T(2,128)(2,1)S(1)}, u32[]{:S(2)}, u32[]{:S(2)}) %all-to-all-start.2) | async-done | bytes 262176 | tf_op jit(solution)/shard_map/all_to_all | solution.py:97
  247.3 7.6 %reshape.356 = bf16[8192,1,16]{2,1,0:T(2,128)(2,1)} reshape(bf16[64,2,1024]{2,1,0:T(2,128)(2,1)S(1)} %all-to-all-done.2) | data formatting | bytes 524288
  254.9 7.9 %copy.143 = bf16[1,16,8192]{2,1,0:T(8,128)(2,1)S(1)} copy(bf16[1,16,8192]{1,0,2:T(2,128)(2,1)} %bitcast.284) | data formatting | bytes 524288 | tf_op jit(solution)/shard_map/all_to_all | solution.py:97
  264.3 6.7 %all-to-all-start.3 = ((bf16[64,16,128]{2,1,0:T(8,128)(2,1)}), bf16[64,16,128]{2,1,0:T(8,128)(2,1)}, u32[]{:S(2)}, u32[]{:S(2)}) async-start(bf16[64,16,128]{2,1,0:T(8,128)(2,1)} %copy.146), calls=%async_computation.4 | async-start | bytes 524288 | tf_op jit(solution)/shard_map/all_to_all | solution.py:114
  271.1 4.3 fusion.51
  276.4 4.8 fusion.49
  281.2 1.5 all-to-all-done.3
  284.9 1.7 fusion.11
  290.7 6.7 %copy.150 = bf16[1,16,8192]{1,0,2:T(2,128)(2,1)} copy(bf16[1,16,8192]{2,1,0:T(8,128)(2,1)S(1)} %convert_element_type.139) | data formatting | bytes 524288 | tf_op jit(solution)/shard_map/convert_element_type | solution.py:98
  297.4 45.6 %reduce.14 = bf16[8192,16]{1,0:T(8,128)(2,1)S(1)} reduce(bf16[8192,1,16]{2,1,0:T(2,128)(2,1)} %bitcast.285, bf16[]{:T(256)} %broadcast.114), dimensions={1}, to_apply=%bitcast.248.reduce_sub_computation | reduce | bytes 524290
  343.0 2.9 reshape.357
  345.9 9.1 %all-to-all-start.4 = ((bf16[64,2,1024]{2,1,0:T(2,128)(2,1)}), bf16[64,2,1024]{2,1,0:T(2,128)(2,1)}, u32[]{:S(2)}, u32[]{:S(2)}) async-start(bf16[64,2,1024]{2,1,0:T(2,128)(2,1)} %reshape.357), calls=%async_computation.5 | async-start | bytes 524288 | tf_op jit(solution)/shard_map/all_to_all | solution.py:97
  355.0 2.6 fusion.69
  357.8 9.1 %all-to-all-done.4 = bf16[64,2,1024]{2,1,0:T(2,128)(2,1)} async-done(((bf16[64,2,1024]{2,1,0:T(2,128)(2,1)}), bf16[64,2,1024]{2,1,0:T(2,128)(2,1)}, u32[]{:S(2)}, u32[]{:S(2)}) %all-to-all-start.4) | async-done | bytes 262176 | tf_op jit(solution)/shard_map/all_to_all | solution.py:97
  366.9 9.8 %reshape.358 = bf16[8192,1,16]{2,1,0:T(2,128)(2,1)} reshape(bf16[64,2,1024]{2,1,0:T(2,128)(2,1)} %all-to-all-done.4) | data formatting | bytes 524288
  376.6 8.6 %copy.151 = bf16[1,16,8192]{2,1,0:T(8,128)(2,1)} copy(bf16[1,16,8192]{1,0,2:T(2,128)(2,1)} %bitcast.286) | data formatting | bytes 524288 | tf_op jit(solution)/shard_map/all_to_all | solution.py:97
  388.4 6.2 %all-to-all-start.5 = ((bf16[64,16,128]{2,1,0:T(8,128)(2,1)}), bf16[64,16,128]{2,1,0:T(8,128)(2,1)}, u32[]{:S(2)}, u32[]{:S(2)}) async-start(bf16[64,16,128]{2,1,0:T(8,128)(2,1)} %copy.152), calls=%async_computation.6 | async-start | bytes 524288 | tf_op jit(solution)/shard_map/all_to_all | solution.py:114
  394.7 7.3 %fusion.52 = f32[256,16,64]{0,2,1:T(8,128)} fusion(f32[256,256]{1,0:T(8,128)} %fusion.111, f32[16,256]{1,0:T(8,128)} %copy-done.22, pred[256,256]{1,0:T(8,128)(4,1)} %iota_compare_fusion, f32[256,16,64]{0,2,1:T(8,128)} %bitcast.318, f32[256,16,64]{0,2,1:T(8,128)S(1)} %bitcast.303, f32[256,16]{0,1:T(8,128)S(1)} %get-tuple-element.35, ...), kind=kOutput, calls=%fused_computation.69 | convolution fusion | flops 810287104 | bytes 3522560 | tf_op jit(solution)/shard_map/hts,shp->thp/dot_general | solution.py:69
  402.1 5.9 %fusion.54 = f32[256,16,64]{0,2,1:T(8,128)} fusion(f32[256,256]{1,0:T(8,128)S(1)} %copy-done.13, f32[16,256]{1,0:T(8,128)S(1)} %copy-done.26, pred[256,256]{1,0:T(8,128)(4,1)S(1)} %copy-done.21, f32[256,16,64]{0,2,1:T(8,128)S(1)} %bitcast.302, f32[256,16,64]{0,2,1:T(8,128)S(1)} %bitcast.316, f32[256,16]{0,1:T(8,128)S(1)} %copy-done.16, ...), kind=kOutput, calls=%fused_computation.71 | convolution fusion | flops 810287104 | bytes 3522560 | tf_op jit(solution)/shard_map/hts,shp->thp/dot_general | solution.py:69
  410.2 1.7 fusion.10
  411.9 5.9 %convolution_convert_fusion = bf16[512,2048]{1,0:T(8,128)(2,1)} fusion(bf16[512,1024]{0,1:T(8,128)(2,1)S(1)} %fusion.10, bf16[1024,2048]{1,0:T(8,128)(2,1)} %param.11), kind=kOutput, calls=%fused_computation.10 | convolution fusion | flops 2148532224 | bytes 7340032 | tf_op jit(solution)/shard_map/dot_general | solution.py:121
  418.6 6.7 %copy.130 = bf16[1,16,8192]{1,0,2:T(2,128)(2,1)} copy(bf16[1,16,8192]{2,1,0:T(8,128)(2,1)S(1)} %convert_element_type.121) | data formatting | bytes 524288 | tf_op jit(solution)/shard_map/convert_element_type | solution.py:98
  425.3 45.5 %reduce.13 = bf16[8192,16]{1,0:T(8,128)(2,1)S(1)} reduce(bf16[8192,1,16]{2,1,0:T(2,128)(2,1)} %bitcast.283, bf16[]{:T(256)} %broadcast.114), dimensions={1}, to_apply=%bitcast.244.reduce_sub_computation | reduce | bytes 524290
  470.7 2.9 reshape.353
  473.7 10.7 %all-to-all-start = ((bf16[64,2,1024]{2,1,0:T(2,128)(2,1)}), bf16[64,2,1024]{2,1,0:T(2,128)(2,1)S(1)}, u32[]{:S(2)}, u32[]{:S(2)}) async-start(bf16[64,2,1024]{2,1,0:T(2,128)(2,1)} %reshape.353), calls=%async_computation | async-start | bytes 524288 | tf_op jit(solution)/shard_map/all_to_all | solution.py:97
  484.4 6.2 %fusion.55 = f32[256,16,64]{0,2,1:T(8,128)S(1)} fusion(f32[256,256]{1,0:T(8,128)S(1)} %copy-done.14, f32[16,256]{1,0:T(8,128)} %copy-done.24, pred[256,256]{1,0:T(8,128)(4,1)} %iota_compare_fusion, f32[256,16,64]{0,2,1:T(8,128)} %bitcast.315, f32[256,16]{0,1:T(8,128)} %copy-done.15, f32[256,16]{0,1:T(8,128)} %get-tuple-element.33, ...), kind=kOutput, calls=%fused_computation.72 | convolution fusion | flops 810549248 | bytes 2998272 | tf_op jit(solution)/shard_map/hts,shp->thp/dot_general | solution.py:69
  490.6 5.6 all-to-all-done
  496.2 7.6 %reshape.354 = bf16[8192,1,16]{2,1,0:T(2,128)(2,1)} reshape(bf16[64,2,1024]{2,1,0:T(2,128)(2,1)S(1)} %all-to-all-done) | data formatting | bytes 524288
  503.8 8.0 %copy.131 = bf16[1,16,8192]{2,1,0:T(8,128)(2,1)S(1)} copy(bf16[1,16,8192]{1,0,2:T(2,128)(2,1)} %bitcast.287) | data formatting | bytes 524288 | tf_op jit(solution)/shard_map/all_to_all | solution.py:97
  514.0 6.0 %all-to-all-start.1 = ((bf16[64,16,128]{2,1,0:T(8,128)(2,1)}), bf16[64,16,128]{2,1,0:T(8,128)(2,1)S(1)}, u32[]{:S(2)}, u32[]{:S(2)}) async-start(bf16[64,16,128]{2,1,0:T(8,128)(2,1)} %copy.134), calls=%async_computation.1 | async-start | bytes 524288 | tf_op jit(solution)/shard_map/all_to_all | solution.py:114
  520.1 1.3 fusion.71
  521.4 6.9 %fusion.53 = f32[256,16,64]{0,2,1:T(8,128)} fusion(f32[256,256]{1,0:T(8,128)} %fusion.111, f32[16,256]{1,0:T(8,128)} %copy-done.22, pred[256,256]{1,0:T(8,128)(4,1)} %iota_compare_fusion, f32[256,16,64]{0,2,1:T(8,128)S(1)} %bitcast.320, f32[256,16]{0,1:T(8,128)S(1)} %get-tuple-element.35, f32[256,16]{0,1:T(8,128)} %get-tuple-element.30, ...), kind=kOutput, calls=%fused_computation.70 | convolution fusion | flops 810549248 | bytes 2998272 | tf_op jit(solution)/shard_map/hts,shp->thp/dot_general | solution.py:69
  528.3 3.7 all-to-all-done.1
  532.6 1.7 fusion.7
  534.2 5.9 %convolution_convert_fusion.1 = bf16[512,2048]{1,0:T(8,128)(2,1)} fusion(bf16[512,1024]{0,1:T(8,128)(2,1)S(1)} %fusion.7, bf16[1024,2048]{1,0:T(8,128)(2,1)} %param.11), kind=kOutput, calls=%fused_computation.11 | convolution fusion | flops 2148532224 | bytes 7340032 | tf_op jit(solution)/shard_map/dot_general | solution.py:121
  540.2 1.3 copy.155
  541.5 28.4 %reduce-scatter.3.cloned.1.call-done = bf16[512,512]{1,0:T(8,128)(2,1)} async-done(((bf16[512,2048]{1,0:T(8,128)(2,1)}), bf16[512,512]{1,0:T(8,128)(2,1)}) %reduce-scatter.3.cloned.1.call-update) | async-done | bytes 524304 | tf_op jit(solution)/shard_map/reduce_scatter | solution.py:122
  (179 shorter events, 43.6 us)
Async XLA Ops:
  7.2 155.2 %all-gather.3.cloned.1.call-start = ((), (), s32[]{:S(2)}) async-start(), calls=%async_computation.9 | async-start | bytes 2621440 | tf_op jit(solution)/shard_map/all_gather | solution.py:165
  11.4 131.6 %copy-start.27 = (f32[16,4]{0,1:T(4,128)}, f32[16,4]{0,1:T(4,128)S(1)}, u32[]{:S(2)}) copy-start(f32[16,4]{0,1:T(4,128)S(1)} %slice.87) | copy-start | bytes 772
  11.6 1.9 copy-start.34
  144.8 11.2 %copy-start.12 = (f32[16,512]{1,0:T(8,128)S(1)}, f32[16,512]{1,0:T(8,128)}, u32[]{:S(2)}) copy-start(f32[16,512]{1,0:T(8,128)} %param.9) | copy-start | bytes 98308
  144.9 12.6 %copy-start.4 = (bf16[512,128]{1,0:T(8,128)(2,1)S(1)}, bf16[512,128]{1,0:T(8,128)(2,1)}, u32[]{:S(2)}) copy-start(bf16[512,128]{1,0:T(8,128)(2,1)} %param.8) | copy-start | bytes 393220
  144.9 12.6 %copy-start.5 = (bf16[512,128]{1,0:T(8,128)(2,1)S(1)}, bf16[512,128]{1,0:T(8,128)(2,1)}, u32[]{:S(2)}) copy-start(bf16[512,128]{1,0:T(8,128)(2,1)} %param.7) | copy-start | bytes 393220
  146.5 0.8 copy-start.38
  147.2 12.0 %copy-start.15 = (f32[256,16]{0,1:T(8,128)}, f32[256,16]{0,1:T(8,128)S(1)}, u32[]{:S(2)}) copy-start(f32[256,16]{0,1:T(8,128)S(1)} %get-tuple-element.36) | copy-start | bytes 49156
  148.3 4.5 copy-start.39
  149.6 3.0 copy-start.35
  152.8 133.8 %copy-start.6 = (bf16[256,1024]{0,1:T(8,128)(2,1)}, bf16[256,1024]{0,1:T(8,128)(2,1)S(1)}, u32[]{:S(2)}) copy-start(bf16[256,1024]{0,1:T(8,128)(2,1)S(1)} %copy.157) | copy-start | bytes 1572868
  153.5 1.9 copy-start.32
  167.6 2.1 copy-start.3
  167.6 2.1 copy-start.36
  167.6 2.1 copy-start.41
  223.2 14.3 %copy-start.28 = (f32[1024]{0:T(1024)S(1)}, f32[1024]{0:T(1024)}, u32[]{:S(2)}) copy-start(f32[1024]{0:T(1024)} %mul.325) | copy-start | bytes 12292
  226.2 21.1 %all-to-all-start.2 = ((bf16[64,2,1024]{2,1,0:T(2,128)(2,1)}), bf16[64,2,1024]{2,1,0:T(2,128)(2,1)S(1)}, u32[]{:S(2)}, u32[]{:S(2)}) async-start(bf16[64,2,1024]{2,1,0:T(2,128)(2,1)} %reshape.355), calls=%async_computation.3 | async-start | bytes 524288 | tf_op jit(solution)/shard_map/all_to_all | solution.py:97
  239.2 23.7 %copy-start.29 = (f32[64,16]{0,1:T(8,128)S(1)}, f32[64,16]{0,1:T(8,128)}, u32[]{:S(2)}) copy-start(f32[64,16]{0,1:T(8,128)} %copy.133) | copy-start | bytes 12292
  239.2 23.7 %copy-start.30 = (f32[64,16]{0,1:T(8,128)S(1)}, f32[64,16]{0,1:T(8,128)}, u32[]{:S(2)}) copy-start(f32[64,16]{0,1:T(8,128)} %copy.132) | copy-start | bytes 12292
  239.2 23.7 %copy-start.31 = (pred[64,64]{1,0:T(8,128)(4,1)S(1)}, pred[64,64]{1,0:T(8,128)(4,1)}, u32[]{:S(2)}) copy-start(pred[64,64]{1,0:T(8,128)(4,1)} %iota_compare_fusion.1) | copy-start | bytes 12292
  254.9 16.1 %copy-start.17 = (f32[256,16]{0,1:T(8,128)S(1)}, f32[256,16]{0,1:T(8,128)}, u32[]{:S(2)}) copy-start(f32[256,16]{0,1:T(8,128)} %get-tuple-element.37) | copy-start | bytes 49156
  254.9 16.1 %copy-start.19 = (f32[256,16]{0,1:T(8,128)S(1)}, f32[256,16]{0,1:T(8,128)}, u32[]{:S(2)}) copy-start(f32[256,16]{0,1:T(8,128)} %get-tuple-element.33) | copy-start | bytes 49156
  254.9 16.1 %copy-start.25 = (f32[16,256]{1,0:T(8,128)S(1)}, f32[16,256]{1,0:T(8,128)}, u32[]{:S(2)}) copy-start(f32[16,256]{1,0:T(8,128)} %copy-done.24) | copy-start | bytes 49156
  264.3 18.4 %all-to-all-start.3 = ((bf16[64,16,128]{2,1,0:T(8,128)(2,1)}), bf16[64,16,128]{2,1,0:T(8,128)(2,1)}, u32[]{:S(2)}, u32[]{:S(2)}) async-start(bf16[64,16,128]{2,1,0:T(8,128)(2,1)} %copy.146), calls=%async_computation.4 | async-start | bytes 524288 | tf_op jit(solution)/shard_map/all_to_all | solution.py:114
  271.1 5.3 copy-start.11
  271.1 5.3 copy-start.18
  271.1 5.3 copy-start.23
  281.2 5.5 copy-start.8
  287.1 2.5 copy-start.33
  287.1 2.5 copy-start.40
  287.8 2.1 copy-start.2
  288.4 1.2 copy-start
  345.9 21.0 %all-to-all-start.4 = ((bf16[64,2,1024]{2,1,0:T(2,128)(2,1)}), bf16[64,2,1024]{2,1,0:T(2,128)(2,1)}, u32[]{:S(2)}, u32[]{:S(2)}) async-start(bf16[64,2,1024]{2,1,0:T(2,128)(2,1)} %reshape.357), calls=%async_computation.5 | async-start | bytes 524288 | tf_op jit(solution)/shard_map/all_to_all | solution.py:97
  388.4 19.6 %all-to-all-start.5 = ((bf16[64,16,128]{2,1,0:T(8,128)(2,1)}), bf16[64,16,128]{2,1,0:T(8,128)(2,1)}, u32[]{:S(2)}, u32[]{:S(2)}) async-start(bf16[64,16,128]{2,1,0:T(8,128)(2,1)} %copy.152), calls=%async_computation.6 | async-start | bytes 524288 | tf_op jit(solution)/shard_map/all_to_all | solution.py:114
  394.6 146.9 %reduce-scatter.5.cloned.1.call-start = ((), (), s32[]{:S(2)}) async-start(), calls=%async_computation.10 | async-start | bytes 2621440 | tf_op jit(solution)/shard_map/reduce_scatter | solution.py:122
  394.7 7.4 %copy-start.10 = (f32[1024,256]{1,0:T(8,128)S(1)}, f32[1024,256]{1,0:T(8,128)}, u32[]{:S(2)}) copy-start(f32[1024,256]{1,0:T(8,128)} %fusion.97) | copy-start | bytes 3145732
  394.7 7.4 %copy-start.13 = (f32[256,256]{1,0:T(8,128)S(1)}, f32[256,256]{1,0:T(8,128)}, u32[]{:S(2)}) copy-start(f32[256,256]{1,0:T(8,128)} %fusion.104) | copy-start | bytes 786436
  394.7 7.4 %copy-start.16 = (f32[256,16]{0,1:T(8,128)S(1)}, f32[256,16]{0,1:T(8,128)}, u32[]{:S(2)}) copy-start(f32[256,16]{0,1:T(8,128)} %copy-done.15) | copy-start | bytes 49156
  394.7 7.4 %copy-start.20 = (f32[256,16]{0,1:T(8,128)S(1)}, f32[256,16]{0,1:T(8,128)}, u32[]{:S(2)}) copy-start(f32[256,16]{0,1:T(8,128)} %get-tuple-element.33) | copy-start | bytes 49156
  394.7 7.4 %copy-start.21 = (pred[256,256]{1,0:T(8,128)(4,1)S(1)}, pred[256,256]{1,0:T(8,128)(4,1)}, u32[]{:S(2)}) copy-start(pred[256,256]{1,0:T(8,128)(4,1)} %iota_compare_fusion) | copy-start | bytes 196612
  394.7 7.4 %copy-start.26 = (f32[16,256]{1,0:T(8,128)S(1)}, f32[16,256]{1,0:T(8,128)}, u32[]{:S(2)}) copy-start(f32[16,256]{1,0:T(8,128)} %copy-done.24) | copy-start | bytes 49156
  402.1 8.1 %copy-start.9 = (f32[256,16,64]{0,2,1:T(8,128)S(1)}, f32[256,16,64]{0,2,1:T(8,128)}, u32[]{:S(2)}) copy-start(f32[256,16,64]{0,2,1:T(8,128)} %fusion.52) | copy-start | bytes 3145732
  425.3 59.1 %copy-start.14 = (f32[256,256]{1,0:T(8,128)S(1)}, f32[256,256]{1,0:T(8,128)}, u32[]{:S(2)}) copy-start(f32[256,256]{1,0:T(8,128)} %fusion.104) | copy-start | bytes 786436
  473.7 22.6 %all-to-all-start = ((bf16[64,2,1024]{2,1,0:T(2,128)(2,1)}), bf16[64,2,1024]{2,1,0:T(2,128)(2,1)S(1)}, u32[]{:S(2)}, u32[]{:S(2)}) async-start(bf16[64,2,1024]{2,1,0:T(2,128)(2,1)} %reshape.353), calls=%async_computation | async-start | bytes 524288 | tf_op jit(solution)/shard_map/all_to_all | solution.py:97
  503.8 16.2 %copy-start.1 = (f32[1024,128]{1,0:T(8,128)S(1)}, f32[1024,128]{1,0:T(8,128)}, u32[]{:S(2)}) copy-start(f32[1024,128]{1,0:T(8,128)} %copy-done) | copy-start | bytes 1572868
  503.8 17.6 %copy-start.7 = (bf16[256,1024]{0,1:T(8,128)(2,1)S(1)}, bf16[256,1024]{0,1:T(8,128)(2,1)}, u32[]{:S(2)}) copy-start(bf16[256,1024]{0,1:T(8,128)(2,1)} %copy-done.6) | copy-start | bytes 1572868
  514.0 18.0 %all-to-all-start.1 = ((bf16[64,16,128]{2,1,0:T(8,128)(2,1)}), bf16[64,16,128]{2,1,0:T(8,128)(2,1)S(1)}, u32[]{:S(2)}, u32[]{:S(2)}) async-start(bf16[64,16,128]{2,1,0:T(8,128)(2,1)} %copy.134), calls=%async_computation.1 | async-start | bytes 524288 | tf_op jit(solution)/shard_map/all_to_all | solution.py:114
  520.0 49.8 %reduce-scatter.3.cloned.1.call-start = ((), (), s32[]{:S(2)}) async-start(), calls=%async_computation.8 | async-start | bytes 2621440 | tf_op jit(solution)/shard_map/reduce_scatter | solution.py:122
  (3 other events, 1.7 us)
Sparse Core Ops, SparseCore 0:
  9.8 37.1 all-gather.2
  418.0 33.2 reduce-scatter.4
  540.3 29.5 reduce-scatter.2
where the time goes:
time: 586 us; the launch traced here: 577 us
  other arithmetic  147 us (25%)
  blocking collectives  128 us (22%)
  local copies, waits for them, and re-layouts  105 us (18%)
  matrix products  75.5 us (13%)
  waiting for transfers between devices  57.2 us (10%)
  starting transfers between devices  47.9 us (8%)
  between operations  15.6 us (3%)
    unnamed x3, other arithmetic  136 us
    unnamed x1, blocking collectives  128 us
    unnamed x100, local copies, waits for them, and re-layouts  40.6 us
    all_to_all x3, starting transfers between devices, carry_incoming(): lax.all_to_all(flattened[None].astype(jnp.bfloat16), 'seq', split_axis=2,...  28.8 us
    reduce_scatter x2, waiting for transfers between devices, head_project(): lax.psum_scatter(partial_value.astype(jnp.bfloat16), 'head', scatter_dime...  28.4 us
    dot_general x4, matrix products, block_forward(): intra_part = jnp.einsum('hts,shp->thp', mixing, driven, precision=highest)  26.4 us
    all_to_all x3, local copies, waits for them, and re-layouts, carry_incoming(): lax.all_to_all(flattened[None].astype(jnp.bfloat16), 'seq', split_axis=2,...  24.5 us
    all_to_all x3, waiting for transfers between devices, carry_incoming(): lax.all_to_all(flattened[None].astype(jnp.bfloat16), 'seq', split_axis=2,...  22.9 us
  transfers between devices with their start and end apart: 9, of which 6 were waited for; matrix products, arithmetic and copies ran while one was open for 26% of the time, Pallas kernels for 0%

commit v1 on v0

v1 whole, which is shorter than its diff:
```python
import functools

import jax
import jax.numpy as jnp
from jax import lax
from jax.experimental import pallas as pl
from jax.experimental.pallas import tpu as pltpu
from jax.sharding import PartitionSpec as P

Q = 256
F32 = jnp.float32
BF = jnp.bfloat16
MESH = pl.DeviceIdType.MESH
CHIPS = 32
LO, HI = slice(0, Q), slice(Q, 2 * Q)


def mm(a, b):
    return jnp.dot(a, b, preferred_element_type=F32)


def mm_nt(a, b):
    return lax.dot_general(a, b, (((1,), (1,)), ((), ())), preferred_element_type=F32)


def kernel(
    x_ref, b_ref, c_ref, ld_ref, sc_ref, w_hbm,
    ch_ref, ig_ref, sg_ref,
    w_v, rise_x, tw_x, bT, cT, cum, g_row, cumT, gT, sco, scoT, mix, mixT, dec,
    yl, vl, mid, end, sin, pulled, mixed, gbuf,
    ep_src, ep_dst, tot, rbuf, pbuf, sbuf, sp_src, sp_dst, dt, dtp, dchip, dall,
    pblk, ropp, from_l, from_r,
    w_sem, ag_s, ag_r, ex_s, ex_r, d_s, d_r, rs_s, rs_r,
):
    s_idx, hx = lax.axis_index("seq"), lax.axis_index("head")
    chip, core = s_idx // 2, lax.rem(s_idx, 2)
    right, left, opp = lax.rem(hx + 1, 4), lax.rem(hx + 3, 4), lax.rem(hx + 2, 4)
    dev_r, dev_l = (s_idx, right), (s_idx, left)
    dev_p = (2 * chip + 1 - core, hx)

    def rcopy(src, dst, ssem, rsem, dev):
        return pltpu.make_async_remote_copy(
            src_ref=src, dst_ref=dst, send_sem=ssem, recv_sem=rsem,
            device_id=dev, device_id_type=MESH,
        )

    barrier = pltpu.get_barrier_semaphore()
    for dev in (dev_r, dev_l, dev_p):
        pl.semaphore_signal(barrier, inc=1, device_id=dev, device_id_type=MESH)

    def greet(o, carry):
        d = lax.rem(chip + o, CHIPS)
        pl.semaphore_signal(barrier, inc=1, device_id=(2 * d + core, hx), device_id_type=MESH)
        return carry

    lax.fori_loop(1, CHIPS, greet, 0)
    w_copy = pltpu.make_async_copy(w_hbm, w_v, w_sem)
    w_copy.start()
    pl.semaphore_wait(barrier, 3 + CHIPS - 1)

    ag = [
        rcopy(sc_ref.at[LO], gbuf.at[hx, LO], ag_s.at[0], ag_r.at[0], dev_r),
        rcopy(sc_ref.at[HI], gbuf.at[hx, HI], ag_s.at[1], ag_r.at[1], dev_l),
        rcopy(sc_ref.at[HI], gbuf.at[hx, HI], ag_s.at[2], ag_r.at[2], dev_r),
        rcopy(sc_ref.at[LO], gbuf.at[hx, LO], ag_s.at[3], ag_r.at[3], dev_l),
        rcopy(gbuf.at[left, LO], gbuf.at[left, LO], ag_s.at[4], ag_r.at[4], dev_r),
        rcopy(gbuf.at[right, HI], gbuf.at[right, HI], ag_s.at[5], ag_r.at[5], dev_l),
    ]
    for copy in ag[:4]:
        copy.start()

    spread = (
        lax.broadcasted_iota(jnp.int32, (16, 1024), 0)
        == lax.shift_right_logical(lax.broadcasted_iota(jnp.int32, (16, 1024), 1), 6)
    ).astype(F32)
    spread_b = spread.astype(BF)
    lane = lax.broadcasted_iota(jnp.int32, (16, Q), 1)
    for blk in range(2):
        at = slice(blk * Q, (blk + 1) * Q)
        ld = ld_ref[:, at]
        y = -2.0 * ld
        series = jnp.ones_like(y)
        for k in range(9, 1, -1):
            series = 1.0 - y * (1.0 / k) * series
        log_w = 0.5 * jnp.log(jnp.where(y < 0.5, y * series, 1.0 - jnp.exp(-y)))
        c = ld
        for k in (1, 2, 4, 8, 16, 32, 64, 128):
            c = c + jnp.where(lane >= k, pltpu.roll(c, k, 1), 0.0)
        total = c[:, Q - 1 : Q]
        g = c - log_w
        cum[:, at] = c
        g_row[:, at] = g
        cumT[at, :] = c.T
        gT[at, :] = g.T
        rise_x[at, :] = mm(jnp.exp(c).T.astype(BF), spread_b).astype(BF)
        tw_x[at, :] = mm(jnp.exp(total - g).T.astype(BF), spread_b).astype(BF)
        dec[blk : blk + 1, :] = jnp.sum(spread * jnp.exp(total), axis=0, keepdims=True)
    d_dev = dec[0:1, :] * dec[1:2, :]
    dec[2:3, :] = d_dev
    for r in range(8):
        dt[r : r + 1, :] = d_dev[:, 128 * r : 128 * r + 128]
    bT[...] = b_ref[...].astype(F32).T.astype(BF)
    cT[...] = c_ref[...].astype(F32).T.astype(BF)
    low = lax.broadcasted_iota(jnp.int32, (Q, Q), 0) >= lax.broadcasted_iota(jnp.int32, (Q, Q), 1)
    high = lax.broadcasted_iota(jnp.int32, (Q, Q), 0) <= lax.broadcasted_iota(jnp.int32, (Q, Q), 1)
    for blk in range(2):
        at = slice(blk * Q, (blk + 1) * Q)
        sco[blk] = jnp.where(low, mm(c_ref[at, :], bT[:, at]), 0.0)
        scoT[blk] = jnp.where(high, mm(b_ref[at, :], cT[:, at]), 0.0)

    def make_table(table, rows_f, cols_f, score):
        def body(g, carry):
            for i in range(2):
                h = 2 * g + i
                onehot = lax.broadcasted_iota(jnp.int32, (Q, 16), 1) == h
                for blk in range(2):
                    at = slice(blk * Q, (blk + 1) * Q)
                    col = jnp.sum(jnp.where(onehot, cols_f[at, :], 0.0), axis=1, keepdims=True)
                    row = rows_f[pl.ds(h, 1), at]
                    gap = col - row if table is mix else row - col
                    value = jnp.exp(jnp.minimum(gap, 0.0)) * score[blk]
                    table[g, blk, :, i * Q : (i + 1) * Q] = value.astype(BF)
            return carry

        lax.fori_loop(0, 8, body, 0)

    lane_a = (lax.broadcasted_iota(jnp.int32, (Q, 128), 1) < 64).astype(F32)
    mask_a, mask_b = lane_a.astype(BF), (1.0 - lane_a).astype(BF)

    def intra(src, table, out):
        def body(g, carry):
            cols = pl.ds(pl.multiple_of(g * 128, 128), 128)
            for blk in range(2):
                at = slice(blk * Q, (blk + 1) * Q)
                z = src[at, cols]
                both = jnp.concatenate([z * mask_a, z * mask_b], axis=0)
                out[at, cols] = mm(table[g, blk], both)
            return carry

        lax.fori_loop(0, 8, body, 0)

    def end_state(k, src, scale, mapT, fwd):
        def body(q, carry):
            cols = pl.ds(pl.multiple_of(q * 256, 256), 256)
            p0 = mm(mapT[:, LO], src[LO, cols] * scale[LO, cols])
            p1 = mm(mapT[:, HI], src[HI, cols] * scale[HI, cols])
            if fwd:
                mid[k, :, cols] = p0
                end[k, :, cols] = dec[1:2, cols] * p0 + p1
            else:
                mid[k, :, cols] = p1
                end[k, :, cols] = dec[0:1, cols] * p1 + p0
            return carry

        lax.fori_loop(0, 4, body, 0)

    def finish(k, rows, local, scale, out, fwd, factor=None):
        def body(q, carry):
            cols = pl.ds(pl.multiple_of(q * 256, 256), 256)
            s = sin[k, :, cols]
            if fwd:
                s0, s1 = s, mid[k, :, cols] + dec[0:1, cols] * s
            else:
                s1, s0 = s, mid[k, :, cols] + dec[1:2, cols] * s
            for at, state in ((LO, s0), (HI, s1)):
                value = local[at, cols] + scale[at, cols].astype(F32) * mm(
                    rows[at, :], state.astype(BF)
                )
                if factor is not None:
                    value = factor * value
                out[at, cols] = value.astype(BF)
            return carry

        lax.fori_loop(0, 4, body, 0)

    mine = pl.ds(pl.multiple_of(core * 512, 512), 512)
    other = pl.ds(pl.multiple_of((1 - core) * 512, 512), 512)
    core_f = core.astype(F32)
    decay_row = 4 * core + lax.rem(chip, 4)

    def spread_out(src, dst, ssem, rsem):
        def body(o, carry):
            d = lax.rem(chip + o, CHIPS)
            rcopy(src.at[d], dst.at[chip], ssem, rsem, (2 * d + core, hx)).start()
            return carry

        lax.fori_loop(1, CHIPS, body, 0)

    def all_of(src, dst, ssem, rsem):
        part = pl.ds(0, CHIPS - 1)
        return rcopy(src.at[part], dst.at[part], ssem, rsem, dev_p)

    waits = []

    def ex_pair(k):
        ep_src[k] = end[k, :, other].astype(BF)
        rcopy(ep_src.at[k], ep_dst.at[k], ex_s.at[k, 0], ex_r.at[k, 0], dev_p).start()
        if k == 0:
            rcopy(dt, dtp, d_s.at[0], d_r.at[0], dev_p).start()

    def ex_out(k, fwd):
        copy = rcopy(ep_src.at[k], ep_dst.at[k], ex_s.at[k, 0], ex_r.at[k, 0], dev_p)
        copy.wait_recv()
        waits.append(copy)
        if k == 0:
            copy = rcopy(dt, dtp, d_s.at[0], d_r.at[0], dev_p)
            copy.wait_recv()
            waits.append(copy)
            dchip[...] = dt[...] * dtp[...]
            for r in range(8):
                dec[3:4, 128 * r : 128 * r + 128] = dtp[r : r + 1, :]
            dall[pl.ds(chip, 1)] = dchip[...][None]

            def body(o, carry):
                d = lax.rem(chip + o, CHIPS)
                rcopy(dchip, dall.at[chip], d_s.at[1], d_r.at[1], (2 * d + core, hx)).start()
                return carry

            lax.fori_loop(1, CHIPS, body, 0)
        first = 1.0 - core_f if fwd else core_f
        d_me, d_p = dec[2:3, mine], dec[3:4, mine]
        value = (1.0 - first + first * d_p) * end[k, :, mine] + (
            first + (1.0 - first) * d_me
        ) * ep_dst[k].astype(F32)
        value = value.astype(BF)
        for i in range(8):
            for j in range(4):
                tot[k, 4 * i + j] = value[16 * i : 16 * i + 16, 128 * j : 128 * j + 128]
        rbuf[k, pl.ds(chip, 1)] = tot[k, pl.ds(chip, 1)]
        spread_out(tot.at[k], rbuf.at[k], ex_s.at[k, 1], ex_r.at[k, 1])

    def ex_back(k, fwd):
        copy = all_of(tot.at[k], rbuf.at[k], ex_s.at[k, 1], ex_r.at[k, 1])
        copy.wait_recv()
        waits.append(copy)
        if k == 0:
            part = pl.ds(0, CHIPS - 1)
            copy = rcopy(dall.at[part], dall.at[part], d_s.at[1], d_r.at[1], dev_p)
            copy.wait_recv()
            waits.append(copy)
        run = jnp.zeros((16, 128), F32)
        for e in range(CHIPS) if fwd else range(CHIPS - 1, -1, -1):
            pbuf[k, e] = run.astype(BF)
            run = run * dall[e, pl.ds(decay_row, 1), :] + rbuf[k, e].astype(F32)
        sbuf[k, pl.ds(chip, 1)] = pbuf[k, pl.ds(chip, 1)]
        spread_out(pbuf.at[k], sbuf.at[k], ex_s.at[k, 2], ex_r.at[k, 2])

    def ex_split(k, fwd):
        copy = all_of(pbuf.at[k], sbuf.at[k], ex_s.at[k, 2], ex_r.at[k, 2])
        copy.wait_recv()
        waits.append(copy)
        first = 1.0 - core_f if fwd else core_f
        for j in range(4):
            cols = pl.ds(pl.multiple_of(core * 512 + 128 * j, 128), 128)
            d_me, d_p = dec[2:3, cols], dec[3:4, cols]
            for i in range(8):
                at = slice(16 * i, 16 * i + 16)
                s = sbuf[k, 4 * i + j].astype(F32)
                theirs = (1.0 - first + first * d_me) * s + first * end[k, at, cols]
                sp_src[k, at, 128 * j : 128 * j + 128] = theirs.astype(BF)
                e_p = ep_dst[k, at, 128 * j : 128 * j + 128].astype(F32)
                sin[k, at, cols] = (first + (1.0 - first) * d_p) * s + (1.0 - first) * e_p
        rcopy(sp_src.at[k], sp_dst.at[k], ex_s.at[k, 3], ex_r.at[k, 3], dev_p).start()

    def ex_end(k):
        copy = rcopy(sp_src.at[k], sp_dst.at[k], ex_s.at[k, 3], ex_r.at[k, 3], dev_p)
        copy.wait_recv()
        waits.append(copy)
        sin[k, :, other] = sp_dst[k].astype(F32)

    def project(r, slot, dest):
        cols = pl.ds(pl.multiple_of(dest * 512, 512), 512)

        def body(i, carry):
            at = pl.ds(pl.multiple_of(i * Q, Q), Q)
            pblk[r, slot, at, :] = mm(mixed[at, :], w_v[:, cols]).astype(BF)
            return carry

        lax.fori_loop(0, 2, body, 0)

    def rs_copies(r):
        return [
            rcopy(pblk.at[r, 0, LO], ropp.at[r, 0], rs_s.at[r, 0], rs_r.at[r, 0], dev_r),
            rcopy(pblk.at[r, 0, HI], ropp.at[r, 1], rs_s.at[r, 1], rs_r.at[r, 1], dev_l),
            rcopy(pblk.at[r, 1, HI], from_l.at[r, HI], rs_s.at[r, 2], rs_r.at[r, 2], dev_r),
            rcopy(pblk.at[r, 2, LO], from_r.at[r, LO], rs_s.at[r, 3], rs_r.at[r, 3], dev_l),
            rcopy(pblk.at[r, 1, LO], from_l.at[r, LO], rs_s.at[r, 4], rs_r.at[r, 4], dev_r),
            rcopy(pblk.at[r, 2, HI], from_r.at[r, HI], rs_s.at[r, 5], rs_r.at[r, 5], dev_l),
        ]

    rs = [rs_copies(0), rs_copies(1)]

    def rs_first(r):
        project(r, 0, opp)
        rs[r][0].start()
        rs[r][1].start()

    def rs_second(r):
        project(r, 1, right)
        rs[r][2].start()
        project(r, 2, left)
        rs[r][3].start()
        project(r, 3, hx)

    def rs_mid(r):
        rs[r][0].wait_recv()
        pblk[r, 1, LO, :] = (pblk[r, 1, LO, :].astype(F32) + ropp[r, 0].astype(F32)).astype(BF)
        rs[r][4].start()
        rs[r][1].wait_recv()
        pblk[r, 2, HI, :] = (pblk[r, 2, HI, :].astype(F32) + ropp[r, 1].astype(F32)).astype(BF)
        rs[r][5].start()

    def rs_end(r, out):
        for copy in rs[r][2:]:
            copy.wait_recv()
        out[...] = (
            pblk[r, 3].astype(F32) + from_l[r].astype(F32) + from_r[r].astype(F32)
        ).astype(BF)

    def pull_first():
        def body(n, carry):
            rows = pl.ds(pl.multiple_of(n * Q, Q), Q)
            total = jnp.zeros((2 * Q, Q), F32)
            for block, dest in ((sc_ref, hx), (gbuf.at[left], left), (gbuf.at[right], right)):
                cols = pl.ds(pl.multiple_of(dest * 512, 512), 512)
                total = total + mm_nt(block[...], w_v[rows, cols])
            vl[:, rows] = total
            return carry

        lax.fori_loop(0, 4, body, 0)

    def pull_last():
        cols = pl.ds(pl.multiple_of(opp * 512, 512), 512)

        def body(n, carry):
            rows = pl.ds(pl.multiple_of(n * Q, Q), Q)
            pulled[:, rows] = (vl[:, rows] + mm_nt(gbuf[opp], w_v[rows, cols])).astype(BF)
            return carry

        lax.fori_loop(0, 4, body, 0)

    end_state(0, x_ref, tw_x, bT, True)
    ex_pair(0)
    make_table(mix, g_row, cumT, sco)
    ex_out(0, True)
    intra(x_ref, mix, yl)
    ex_back(0, True)
    make_table(mixT, cum, gT, scoT)
    ex_split(0, True)
    ag[0].wait_recv()
    ag[4].start()
    ag[1].wait_recv()
    ag[5].start()
    ag[2].wait_recv()
    ag[3].wait_recv()
    w_copy.wait()
    pull_first()
    ex_end(0)
    finish(0, c_ref, yl, rise_x, mixed, True)
    ag[4].wait_recv()
    ag[5].wait_recv()
    pull_last()
    end_state(1, pulled, rise_x, cT, False)
    ex_pair(1)
    rs_first(0)
    ex_out(1, False)
    rs_second(0)
    ex_back(1, False)
    intra(pulled, mixT, vl)
    ex_split(1, False)
    rs_mid(0)
    ex_end(1)
    finish(1, b_ref, vl, tw_x, ig_ref, False)
    end_state(2, ig_ref, tw_x, bT, True)
    ex_pair(2)
    intra(ig_ref, mix, yl)
    ex_out(2, True)
    rs_end(0, ch_ref)
    ex_back(2, True)
    ex_split(2, True)
    ex_end(2)
    finish(2, c_ref, yl, rise_x, mixed, True, 2.0)
    rs_first(1)
    rs_second(1)
    rs_mid(1)
    rs_end(1, sg_ref)
    for copy in waits + ag + rs[0] + rs[1]:
        copy.wait_send()


def local(inputs, rows_b, rows_c, log_decay, score_cotangent, out_weight):
    vm = pltpu.VMEM
    dma = pltpu.SemaphoreType.DMA
    scratch = [
        vm((1024, 2048), BF), vm((512, 1024), BF), vm((512, 1024), BF),
        vm((128, 512), BF), vm((128, 512), BF),
        vm((16, 512), F32), vm((16, 512), F32), vm((512, 16), F32), vm((512, 16), F32),
        vm((2, Q, Q), F32), vm((2, Q, Q), F32),
        vm((8, 2, Q, 2 * Q), BF), vm((8, 2, Q, 2 * Q), BF), vm((8, 1024), F32),
        vm((512, 1024), F32), vm((512, 1024), F32),
        vm((3, 128, 1024), F32), vm((3, 128, 1024), F32), vm((3, 128, 1024), F32),
        vm((512, 1024), BF), vm((512, 1024), BF), vm((4, 512, 512), BF),
        vm((3, 128, 512), BF), vm((3, 128, 512), BF),
        vm((3, CHIPS, 16, 128), BF), vm((3, CHIPS, 16, 128), BF),
        vm((3, CHIPS, 16, 128), BF), vm((3, CHIPS, 16, 128), BF),
        vm((3, 128, 512), BF), vm((3, 128, 512), BF),
        vm((8, 128), F32), vm((8, 128), F32), vm((8, 128), F32), vm((CHIPS, 8, 128), F32),
        vm((2, 4, 512, 512), BF), vm((2, 2, Q, 512), BF),
        vm((2, 512, 512), BF), vm((2, 512, 512), BF),
        dma, dma((6,)), dma((6,)), dma((3, 4)), dma((3, 4)), dma((2,)), dma((2,)),
        dma((2, 6)), dma((2, 6)),
    ]
    spec = pl.BlockSpec(memory_space=vm)
    return pl.pallas_call(
        kernel,
        out_shape=(
            jax.ShapeDtypeStruct((512, 512), BF),
            jax.ShapeDtypeStruct((512, 1024), BF),
            jax.ShapeDtypeStruct((512, 512), BF),
        ),
        in_specs=[spec] * 5 + [pl.BlockSpec(memory_space=pl.ANY)],
        out_specs=(spec, spec, spec),
        scratch_shapes=scratch,
        compiler_params=pltpu.CompilerParams(
            collective_id=0, has_side_effects=True, vmem_limit_bytes=58 * 1024 * 1024
        ),
        cost_estimate=pl.CostEstimate(flops=8 * 10**9, bytes_accessed=10**7, transcendentals=0),
    )(inputs, rows_b, rows_c, log_decay, score_cotangent, out_weight)


def solution(mesh):
    return jax.shard_map(
        local,
        mesh=mesh,
        in_specs=(
            P("seq", "head"),
            P("seq", None),
            P("seq", None),
            P("head", "seq"),
            P("seq", "head"),
            P("head", None),
        ),
        out_specs=(P("seq", "head"), P("seq", "head"), P("seq", "head")),
        check_vma=False,
    )
```

time: 586 us -> 108 us (0.18); the launches traced: 577 us -> 107 us
  other arithmetic: 147 us -> 0 us
  blocking collectives: 128 us -> 0 us
  Pallas kernels: 0 us -> 101 us
  local copies, waits for them, and re-layouts: 105 us -> 6 us
  matrix products: 75.5 us -> 0 us
  waiting for transfers between devices: 57.2 us -> 0 us
  starting transfers between devices: 47.9 us -> 0 us
  between operations: 15.6 us -> 0.64 us
    unnamed x3 -> x0, other arithmetic: 136 us -> none
    unnamed x1 -> x0, blocking collectives: 128 us -> none
    pallas_call x0 -> x1, Pallas kernels: none -> 101 us  [local(): pl.pallas_call(kernel, out_shape=(jax.ShapeDtypeStruct((512, 512), BF), j...]
    dot_general x28 -> x0, matrix products: 75.5 us -> none  [the longest x4 26.4 us: block_forward(): intra_part = jnp.einsum('hts,shp->thp', mixing, driven, precision=highest)]
    all_to_all x6 -> x0, starting transfers between devices: 47.8 us -> none  [the longest x3 28.8 us: carry_incoming(): lax.all_to_all(flattened[None].astype(jnp.bfloat16), 'seq', split_axis=2,...]
    unnamed x100 -> x3, local copies, waits for them, and re-layouts: 40.6 us -> 6 us
    reduce_scatter x2 -> x0, waiting for transfers between devices: 28.4 us -> none  [head_project(): lax.psum_scatter(partial_value.astype(jnp.bfloat16), 'head', scatter_dime...]
    all_to_all x6 -> x0, waiting for transfers between devices: 28.1 us -> none  [the longest x3 22.9 us: carry_incoming(): lax.all_to_all(flattened[None].astype(jnp.bfloat16), 'seq', split_axis=2,...]
  transfers between devices with their start and end apart: 9 -> 0, of which waited for: 6 -> 0; matrix products, arithmetic and copies ran while one was open for 26% -> 0% of each run, Pallas kernels for 0% -> 0%
where the time goes in v1:
time: 108 us; the launch traced here: 107 us
  Pallas kernels  101 us (94%)
  local copies, waits for them, and re-layouts  6 us (6%)
    pallas_call x1, Pallas kernels, local(): pl.pallas_call(kernel, out_shape=(jax.ShapeDtypeStruct((512, 512), BF), j...  101 us
    unnamed x3, local copies, waits for them, and re-layouts  6 us

profile of v1, /device:TPU:1, one launch (start us, length us, event | category | flops | bytes accessed | tf_op | source)
XLA Modules:
  0.0 107.4 jit_solution(10746522320836593954)
XLA Ops:
  0.6 100.8 %shard_map.85 = (bf16[512,512]{1,0:T(8,128)(2,1)}, bf16[512,1024]{1,0:T(8,128)(2,1)}, bf16[512,512]{1,0:T(8,128)(2,1)}) custom-call(bf16[512,1024]{1,0:T(8,128)(2,1)} %x_ref.1, bf16[512,128]{1,0:T(8,128)(2,1)} %b_ref.1, bf16[512,128]{1,0:T(8,128)(2,1)} %c_ref.1, f32[16,512]{1,0:T(8,128)} %ld_ref.1, bf16[512,512]{1,0:T(8,128)(2,1)} %sc_ref.1, ...), custom_call_target="tpu_custom_call" | custom-call | flops 8000000000 | bytes 10000000 | tf_op jit(solution)/shard_map/pallas_call | solution.py:414
  101.4 1.9 %copy.12 = bf16[512,512]{1,0:T(8,128)(2,1)} copy(bf16[512,512]{1,0:T(8,128)(2,1)} %get-tuple-element.6) | data formatting | bytes 1048576
  103.3 2.3 %copy.13 = bf16[512,1024]{1,0:T(8,128)(2,1)} copy(bf16[512,1024]{1,0:T(8,128)(2,1)} %get-tuple-element.7) | data formatting | bytes 2097152
  105.6 1.9 %copy.14 = bf16[512,512]{1,0:T(8,128)(2,1)} copy(bf16[512,512]{1,0:T(8,128)(2,1)} %get-tuple-element.8) | data formatting | bytes 1048576

commit v2 on v1

--- a/solution.py
+++ b/solution.py
@@ -24,13 +24,13 @@
 
 
 def kernel(
-    x_ref, b_ref, c_ref, ld_ref, sc_ref, w_hbm,
-    ch_ref, ig_ref, sg_ref,
-    w_v, rise_x, tw_x, bT, cT, cum, g_row, cumT, gT, sco, scoT, mix, mixT, dec,
+    x_hbm, b_hbm, c_hbm, ld_hbm, sc_hbm, w_hbm,
+    ch_hbm, ig_hbm, sg_hbm,
+    x_ref, b_ref, c_ref, ld_ref, sc_ref, ch_ref, ig_ref, sg_ref, w_v, rise_x, tw_x, bT, cT, cum, g_row, cumT, gT, sco, scoT, mix, mixT, dec,
     yl, vl, mid, end, sin, pulled, mixed, gbuf,
     ep_src, ep_dst, tot, rbuf, pbuf, sbuf, sp_src, sp_dst, dt, dtp, dchip, dall,
     pblk, ropp, from_l, from_r,
-    w_sem, ag_s, ag_r, ex_s, ex_r, d_s, d_r, rs_s, rs_r,
+    in_sem, out_sem, round_sem, ag_s, ag_r, ex_s, ex_r, d_s, d_r, rs_s, rs_r,
 ):
     s_idx, hx = lax.axis_index("seq"), lax.axis_index("head")
     chip, core = s_idx // 2, lax.rem(s_idx, 2)
@@ -44,19 +44,37 @@
             device_id=dev, device_id_type=MESH,
         )
 
+    y, z = chip // 8, lax.rem(chip, 8)
+
+    def along_z(o):
+        return (2 * (8 * y + lax.rem(z + o, 8)) + core, hx)
+
+    def along_y(o):
+        return (2 * (8 * lax.rem(y + o, 4) + z) + core, hx)
+
     barrier = pltpu.get_barrier_semaphore()
-    for dev in (dev_r, dev_l, dev_p):
+    for dev in (dev_r, dev_l, dev_p, along_z(1), along_z(7), along_y(1), along_y(3)):
         pl.semaphore_signal(barrier, inc=1, device_id=dev, device_id_type=MESH)
-
-    def greet(o, carry):
-        d = lax.rem(chip + o, CHIPS)
-        pl.semaphore_signal(barrier, inc=1, device_id=(2 * d + core, hx), device_id_type=MESH)
-        return carry
-
-    lax.fori_loop(1, CHIPS, greet, 0)
-    w_copy = pltpu.make_async_copy(w_hbm, w_v, w_sem)
-    w_copy.start()
-    pl.semaphore_wait(barrier, 3 + CHIPS - 1)
+    loads = [
+        pltpu.make_async_copy(src, dst, in_sem.at[i])
+        for i, (src, dst) in enumerate(
+            (
+                (sc_hbm, sc_ref), (ld_hbm, ld_ref), (b_hbm, b_ref),
+                (c_hbm, c_ref), (x_hbm, x_ref), (w_hbm, w_v),
+            )
+        )
+    ]
+    for copy in loads:
+        copy.start()
+    loads[0].wait()
+    pl.semaphore_wait(barrier, 7)
+
+    def tell(i, devs):
+        for dev in devs:
+            pl.semaphore_signal(round_sem.at[i], inc=1, device_id=dev, device_id_type=MESH)
+
+    def heard(i):
+        pl.semaphore_wait(round_sem.at[i], 2)
 
     ag = [
         rcopy(sc_ref.at[LO], gbuf.at[hx, LO], ag_s.at[0], ag_r.at[0], dev_r),
@@ -68,6 +86,9 @@
     ]
     for copy in ag[:4]:
         copy.start()
+    tell(0, (along_z(1), along_z(7)))
+    for copy in loads[1:4]:
+        copy.wait()
 
     spread = (
         lax.broadcasted_iota(jnp.int32, (16, 1024), 0)
@@ -78,11 +99,11 @@
     for blk in range(2):
         at = slice(blk * Q, (blk + 1) * Q)
         ld = ld_ref[:, at]
-        y = -2.0 * ld
-        series = jnp.ones_like(y)
+        u = -2.0 * ld
+        series = jnp.ones_like(u)
         for k in range(9, 1, -1):
-            series = 1.0 - y * (1.0 / k) * series
-        log_w = 0.5 * jnp.log(jnp.where(y < 0.5, y * series, 1.0 - jnp.exp(-y)))
+            series = 1.0 - u * (1.0 / k) * series
+        log_w = 0.5 * jnp.log(jnp.where(u < 0.5, u * series, 1.0 - jnp.exp(-u)))
         c = ld
         for k in (1, 2, 4, 8, 16, 32, 64, 128):
             c = c + jnp.where(lane >= k, pltpu.roll(c, k, 1), 0.0)
@@ -95,6 +116,8 @@
         rise_x[at, :] = mm(jnp.exp(c).T.astype(BF), spread_b).astype(BF)
         tw_x[at, :] = mm(jnp.exp(total - g).T.astype(BF), spread_b).astype(BF)
         dec[blk : blk + 1, :] = jnp.sum(spread * jnp.exp(total), axis=0, keepdims=True)
+    heard(0)
+    tell(1, (along_z(2), along_z(6)))
     d_dev = dec[0:1, :] * dec[1:2, :]
     dec[2:3, :] = d_dev
     for r in range(8):
@@ -178,13 +201,19 @@
     core_f = core.astype(F32)
     decay_row = 4 * core + lax.rem(chip, 4)
 
+    def far_first(o):
+        j, k = o // 8, lax.rem(o, 8)
+        dz = 4 + (k // 2) - lax.rem(k, 2) * (k // 2 + (k + 1) // 2)
+        dy = 2 + (j // 2) - lax.rem(j, 2) * (j // 2 + (j + 1) // 2)
+        return 8 * lax.rem(y + dy, 4) + lax.rem(z + dz, 8)
+
     def spread_out(src, dst, ssem, rsem):
         def body(o, carry):
-            d = lax.rem(chip + o, CHIPS)
+            d = far_first(o)
             rcopy(src.at[d], dst.at[chip], ssem, rsem, (2 * d + core, hx)).start()
             return carry
 
-        lax.fori_loop(1, CHIPS, body, 0)
+        lax.fori_loop(0, CHIPS - 1, body, 0)
 
     def all_of(src, dst, ssem, rsem):
         part = pl.ds(0, CHIPS - 1)
@@ -212,11 +241,11 @@
             dall[pl.ds(chip, 1)] = dchip[...][None]
 
             def body(o, carry):
-                d = lax.rem(chip + o, CHIPS)
+                d = far_first(o)
                 rcopy(dchip, dall.at[chip], d_s.at[1], d_r.at[1], (2 * d + core, hx)).start()
                 return carry
 
-            lax.fori_loop(1, CHIPS, body, 0)
+            lax.fori_loop(0, CHIPS - 1, body, 0)
         first = 1.0 - core_f if fwd else core_f
         d_me, d_p = dec[2:3, mine], dec[3:4, mine]
         value = (1.0 - first + first * d_p) * end[k, :, mine] + (
@@ -268,15 +297,9 @@
         waits.append(copy)
         sin[k, :, other] = sp_dst[k].astype(F32)
 
-    def project(r, slot, dest):
+    def project(r, slot, dest, at):
         cols = pl.ds(pl.multiple_of(dest * 512, 512), 512)
-
-        def body(i, carry):
-            at = pl.ds(pl.multiple_of(i * Q, Q), Q)
-            pblk[r, slot, at, :] = mm(mixed[at, :], w_v[:, cols]).astype(BF)
-            return carry
-
-        lax.fori_loop(0, 2, body, 0)
+        pblk[r, slot, at, :] = mm(mixed[at, :], w_v[:, cols]).astype(BF)
 
     def rs_copies(r):
         return [
@@ -291,16 +314,20 @@
     rs = [rs_copies(0), rs_copies(1)]
 
     def rs_first(r):
-        project(r, 0, opp)
+        project(r, 0, opp, LO)
         rs[r][0].start()
+        project(r, 0, opp, HI)
         rs[r][1].start()
 
     def rs_second(r):
-        project(r, 1, right)
+        project(r, 1, right, HI)
         rs[r][2].start()
-        project(r, 2, left)
+        project(r, 2, left, LO)
         rs[r][3].start()
-        project(r, 3, hx)
+        project(r, 1, right, LO)
+        project(r, 2, left, HI)
+        project(r, 3, hx, LO)
+        project(r, 3, hx, HI)
 
     def rs_mid(r):
         rs[r][0].wait_recv()
@@ -339,9 +366,19 @@
 
         lax.fori_loop(0, 4, body, 0)
 
+    stores = [
+        pltpu.make_async_copy(src, dst, out_sem.at[i])
+        for i, (src, dst) in enumerate(((ch_ref, ch_hbm), (ig_ref, ig_hbm), (sg_ref, sg_hbm)))
+    ]
+    heard(1)
+    tell(2, (along_y(1), along_y(3)))
+    loads[4].wait()
     end_state(0, x_ref, tw_x, bT, True)
     ex_pair(0)
+    heard(2)
+    tell(3, (along_y(1), along_y(3)))
     make_table(mix, g_row, cumT, sco)
+    heard(3)
     ex_out(0, True)
     intra(x_ref, mix, yl)
     ex_back(0, True)
@@ -353,7 +390,7 @@
     ag[5].start()
     ag[2].wait_recv()
     ag[3].wait_recv()
-    w_copy.wait()
+    loads[5].wait()
     pull_first()
     ex_end(0)
     finish(0, c_ref, yl, rise_x, mixed, True)
@@ -371,11 +408,13 @@
     rs_mid(0)
     ex_end(1)
     finish(1, b_ref, vl, tw_x, ig_ref, False)
+    stores[1].start()
     end_state(2, ig_ref, tw_x, bT, True)
     ex_pair(2)
     intra(ig_ref, mix, yl)
     ex_out(2, True)
     rs_end(0, ch_ref)
+    stores[0].start()
     ex_back(2, True)
     ex_split(2, True)
     ex_end(2)
@@ -384,14 +423,28 @@
     rs_second(1)
     rs_mid(1)
     rs_end(1, sg_ref)
+    stores[2].start()
     for copy in waits + ag + rs[0] + rs[1]:
         copy.wait_send()
+    for copy in stores:
+        copy.wait()
+
+
+def hand_on(*refs):
+    sems = refs[6]
+    copies = [pltpu.make_async_copy(refs[i], refs[3 + i], sems.at[i]) for i in range(3)]
+    for copy in copies:
+        copy.start()
+    for copy in copies:
+        copy.wait()
 
 
 def local(inputs, rows_b, rows_c, log_decay, score_cotangent, out_weight):
     vm = pltpu.VMEM
     dma = pltpu.SemaphoreType.DMA
     scratch = [
+        vm((512, 1024), BF), vm((512, 128), BF), vm((512, 128), BF), vm((16, 512), F32),
+        vm((512, 512), BF), vm((512, 512), BF), vm((512, 1024), BF), vm((512, 512), BF),
         vm((1024, 2048), BF), vm((512, 1024), BF), vm((512, 1024), BF),
         vm((128, 512), BF), vm((128, 512), BF),
         vm((16, 512), F32), vm((16, 512), F32), vm((512, 16), F32), vm((512, 16), F32),
@@ -407,25 +460,34 @@
         vm((8, 128), F32), vm((8, 128), F32), vm((8, 128), F32), vm((CHIPS, 8, 128), F32),
         vm((2, 4, 512, 512), BF), vm((2, 2, Q, 512), BF),
         vm((2, 512, 512), BF), vm((2, 512, 512), BF),
-        dma, dma((6,)), dma((6,)), dma((3, 4)), dma((3, 4)), dma((2,)), dma((2,)),
+        dma((6,)), dma((3,)), pltpu.SemaphoreType.REGULAR((4,)), dma((6,)), dma((6,)), dma((3, 4)), dma((3, 4)), dma((2,)), dma((2,)),
         dma((2, 6)), dma((2, 6)),
     ]
-    spec = pl.BlockSpec(memory_space=vm)
-    return pl.pallas_call(
+    spec = pl.BlockSpec(memory_space=pl.ANY)
+    shapes = (
+        jax.ShapeDtypeStruct((512, 512), BF),
+        jax.ShapeDtypeStruct((512, 1024), BF),
+        jax.ShapeDtypeStruct((512, 512), BF),
+    )
+    outs = pl.pallas_call(
         kernel,
-        out_shape=(
-            jax.ShapeDtypeStruct((512, 512), BF),
-            jax.ShapeDtypeStruct((512, 1024), BF),
-            jax.ShapeDtypeStruct((512, 512), BF),
-        ),
-        in_specs=[spec] * 5 + [pl.BlockSpec(memory_space=pl.ANY)],
-        out_specs=(spec, spec, spec),
+        out_shape=shapes,
+        in_specs=[pl.BlockSpec(memory_space=pltpu.HBM)] * 6,
+        out_specs=(spec,) * 3,
         scratch_shapes=scratch,
         compiler_params=pltpu.CompilerParams(
             collective_id=0, has_side_effects=True, vmem_limit_bytes=58 * 1024 * 1024
         ),
         cost_estimate=pl.CostEstimate(flops=8 * 10**9, bytes_accessed=10**7, transcendentals=0),
     )(inputs, rows_b, rows_c, log_decay, score_cotangent, out_weight)
+    return pl.pallas_call(
+        hand_on,
+        out_shape=shapes,
+        in_specs=[pl.BlockSpec(memory_space=vm)] * 3,
+        out_specs=(spec,) * 3,
+        scratch_shapes=[dma((3,))],
+        cost_estimate=pl.CostEstimate(flops=0, bytes_accessed=4 * 2**20, transcendentals=0),
+    )(*outs)
 
 
 def solution(mesh):

time: 108 us -> 99.6 us (0.922)
  local copies, waits for them, and re-layouts: 6 us -> 0 us
  Pallas kernels: 101 us -> 98.8 us
    unnamed x3 -> x0, local copies, waits for them, and re-layouts: 6 us -> none
    pallas_call x1 -> x2, Pallas kernels: 101 us -> 98.8 us  [the longest x1 96 us: local(): pl.pallas_call(kernel, out_shape=shapes, in_specs=[pl.BlockSpec(memory_sp...]
where the time goes in v2:
time: 99.6 us; the launch traced here: 99.5 us
  Pallas kernels  98.8 us (99%)
    pallas_call x1, Pallas kernels, local(): pl.pallas_call(kernel, out_shape=shapes, in_specs=[pl.BlockSpec(memory_sp...  96 us
    pallas_call x1, Pallas kernels, local(): pl.pallas_call(hand_on, out_shape=shapes, in_specs=[pl.BlockSpec(memory_s...  2.85 us

profile of v2, /device:TPU:1, one launch (start us, length us, event | category | flops | bytes accessed | tf_op | source)
XLA Modules:
  0.0 99.5 jit_solution(8411420047120582953)
XLA Ops:
  0.6 96.0 %shard_map.85 = (bf16[512,512]{1,0:T(8,128)(2,1)}, bf16[512,1024]{1,0:T(8,128)(2,1)}, bf16[512,512]{1,0:T(8,128)(2,1)}) custom-call(bf16[512,1024]{1,0:T(8,128)(2,1)} %x_hbm.1, bf16[512,128]{1,0:T(8,128)(2,1)} %b_hbm.1, bf16[512,128]{1,0:T(8,128)(2,1)} %c_hbm.1, f32[16,512]{1,0:T(8,128)} %ld_hbm.1, bf16[512,512]{1,0:T(8,128)(2,1)} %sc_hbm.1, ...), custom_call_target="tpu_custom_call" | custom-call | flops 8000000000 | bytes 10000000 | tf_op jit(solution)/shard_map/pallas_call | solution.py:472
  96.6 2.9 %shard_map.86 = (bf16[512,512]{1,0:T(8,128)(2,1)}, bf16[512,1024]{1,0:T(8,128)(2,1)}, bf16[512,512]{1,0:T(8,128)(2,1)}) custom-call(bf16[512,512]{1,0:T(8,128)(2,1)} %get-tuple-element.6.refs_0_, bf16[512,1024]{1,0:T(8,128)(2,1)} %get-tuple-element.7.refs_1_, bf16[512,512]{1,0:T(8,128)(2,1)} %get-tuple-element.8.refs_2_), custom_call_target="tpu_custom_call" | custom-call | bytes 4194304 | tf_op jit(solution)/shard_map/pallas_call | solution.py:483

commit v3 on v2

--- a/solution.py
+++ b/solution.py
@@ -64,7 +64,7 @@
             )
         )
     ]
-    for copy in loads:
+    for copy in loads[:5]:
         copy.start()
     loads[0].wait()
     pl.semaphore_wait(barrier, 7)
@@ -86,6 +86,7 @@
     ]
     for copy in ag[:4]:
         copy.start()
+    loads[5].start()
     tell(0, (along_z(1), along_z(7)))
     for copy in loads[1:4]:
         copy.wait()
@@ -162,9 +163,9 @@
 
         lax.fori_loop(0, 8, body, 0)
 
-    def end_state(k, src, scale, mapT, fwd):
+    def end_state(k, src, scale, mapT, fwd, base):
         def body(q, carry):
-            cols = pl.ds(pl.multiple_of(q * 256, 256), 256)
+            cols = pl.ds(pl.multiple_of(base + q * 256, 256), 256)
             p0 = mm(mapT[:, LO], src[LO, cols] * scale[LO, cols])
             p1 = mm(mapT[:, HI], src[HI, cols] * scale[HI, cols])
             if fwd:
@@ -175,11 +176,11 @@
                 end[k, :, cols] = dec[0:1, cols] * p1 + p0
             return carry
 
-        lax.fori_loop(0, 4, body, 0)
-
-    def finish(k, rows, local, scale, out, fwd, factor=None):
+        lax.fori_loop(0, 2, body, 0)
+
+    def finish(k, rows, local, scale, out, fwd, base, factor=None):
         def body(q, carry):
-            cols = pl.ds(pl.multiple_of(q * 256, 256), 256)
+            cols = pl.ds(pl.multiple_of(base + q * 256, 256), 256)
             s = sin[k, :, cols]
             if fwd:
                 s0, s1 = s, mid[k, :, cols] + dec[0:1, cols] * s
@@ -194,10 +195,11 @@
                 out[at, cols] = value.astype(BF)
             return carry
 
-        lax.fori_loop(0, 4, body, 0)
-
-    mine = pl.ds(pl.multiple_of(core * 512, 512), 512)
-    other = pl.ds(pl.multiple_of((1 - core) * 512, 512), 512)
+        lax.fori_loop(0, 2, body, 0)
+
+    near, far = core * 512, (1 - core) * 512
+    mine = pl.ds(pl.multiple_of(near, 512), 512)
+    other = pl.ds(pl.multiple_of(far, 512), 512)
     core_f = core.astype(F32)
     decay_row = 4 * core + lax.rem(chip, 4)
 
@@ -356,34 +358,32 @@
 
         lax.fori_loop(0, 4, body, 0)
 
-    def pull_last():
+    def pull_last(base):
         cols = pl.ds(pl.multiple_of(opp * 512, 512), 512)
 
         def body(n, carry):
-            rows = pl.ds(pl.multiple_of(n * Q, Q), Q)
+            rows = pl.ds(pl.multiple_of(base + n * Q, Q), Q)
             pulled[:, rows] = (vl[:, rows] + mm_nt(gbuf[opp], w_v[rows, cols])).astype(BF)
             return carry
 
-        lax.fori_loop(0, 4, body, 0)
+        lax.fori_loop(0, 2, body, 0)
 
     stores = [
         pltpu.make_async_copy(src, dst, out_sem.at[i])
         for i, (src, dst) in enumerate(((ch_ref, ch_hbm), (ig_ref, ig_hbm), (sg_ref, sg_hbm)))
     ]
+    loads[4].wait()
+    end_state(0, x_ref, tw_x, bT, True, far)
+    end_state(0, x_ref, tw_x, bT, True, near)
+    ex_pair(0)
     heard(1)
     tell(2, (along_y(1), along_y(3)))
-    loads[4].wait()
-    end_state(0, x_ref, tw_x, bT, True)
-    ex_pair(0)
+    make_table(mix, g_row, cumT, sco)
     heard(2)
     tell(3, (along_y(1), along_y(3)))
-    make_table(mix, g_row, cumT, sco)
+    make_table(mixT, cum, gT, scoT)
     heard(3)
     ex_out(0, True)
-    intra(x_ref, mix, yl)
-    ex_back(0, True)
-    make_table(mixT, cum, gT, scoT)
-    ex_split(0, True)
     ag[0].wait_recv()
     ag[4].start()
     ag[1].wait_recv()
@@ -392,33 +392,42 @@
     ag[3].wait_recv()
     loads[5].wait()
     pull_first()
-    ex_end(0)
-    finish(0, c_ref, yl, rise_x, mixed, True)
+    ex_back(0, True)
     ag[4].wait_recv()
     ag[5].wait_recv()
-    pull_last()
-    end_state(1, pulled, rise_x, cT, False)
+    pull_last(far)
+    end_state(1, pulled, rise_x, cT, False, far)
     ex_pair(1)
+    pull_last(near)
+    end_state(1, pulled, rise_x, cT, False, near)
+    ex_out(1, False)
+    intra(x_ref, mix, yl)
+    ex_split(0, True)
+    finish(0, c_ref, yl, rise_x, mixed, True, near)
+    ex_end(0)
+    finish(0, c_ref, yl, rise_x, mixed, True, far)
     rs_first(0)
-    ex_out(1, False)
+    ex_back(1, False)
     rs_second(0)
-    ex_back(1, False)
     intra(pulled, mixT, vl)
     ex_split(1, False)
+    finish(1, b_ref, vl, tw_x, ig_ref, False, near)
+    end_state(2, ig_ref, tw_x, bT, True, near)
+    ex_end(1)
+    finish(1, b_ref, vl, tw_x, ig_ref, False, far)
+    end_state(2, ig_ref, tw_x, bT, True, far)
+    ex_pair(2)
     rs_mid(0)
-    ex_end(1)
-    finish(1, b_ref, vl, tw_x, ig_ref, False)
+    ex_out(2, True)
     stores[1].start()
-    end_state(2, ig_ref, tw_x, bT, True)
-    ex_pair(2)
     intra(ig_ref, mix, yl)
-    ex_out(2, True)
+    ex_back(2, True)
     rs_end(0, ch_ref)
     stores[0].start()
-    ex_back(2, True)
     ex_split(2, True)
+    finish(2, c_ref, yl, rise_x, mixed, True, near, 2.0)
     ex_end(2)
-    finish(2, c_ref, yl, rise_x, mixed, True, 2.0)
+    finish(2, c_ref, yl, rise_x, mixed, True, far, 2.0)
     rs_first(1)
     rs_second(1)
     rs_mid(1)
@@ -431,11 +440,16 @@
 
 
 def hand_on(*refs):
-    sems = refs[6]
-    copies = [pltpu.make_async_copy(refs[i], refs[3 + i], sems.at[i]) for i in range(3)]
-    for copy in copies:
+    sources, results, held, in_sem, out_sem = refs[:3], refs[3:6], refs[6:9], refs[9], refs[10]
+    order = (1, 0, 2)
+    loads = [pltpu.make_async_copy(sources[i], held[i], in_sem.at[i]) for i in order]
+    stores = [pltpu.make_async_copy(held[i], results[i], out_sem.at[i]) for i in order]
+    for copy in loads:
         copy.start()
-    for copy in copies:
+    for load, store in zip(loads, stores):
+        load.wait()
+        store.start()
+    for copy in stores:
         copy.wait()
 
 
@@ -483,9 +497,10 @@
     return pl.pallas_call(
         hand_on,
         out_shape=shapes,
-        in_specs=[pl.BlockSpec(memory_space=vm)] * 3,
+        in_specs=[pl.BlockSpec(memory_space=pltpu.HBM)] * 3,
         out_specs=(spec,) * 3,
-        scratch_shapes=[dma((3,))],
+        scratch_shapes=[vm((512, 512), BF), vm((512, 1024), BF), vm((512, 512), BF)]
+        + [dma((3,)), dma((3,))],
         cost_estimate=pl.CostEstimate(flops=0, bytes_accessed=4 * 2**20, transcendentals=0),
     )(*outs)
 

time: 99.6 us -> 87 us (0.87)
  Pallas kernels: 98.8 us -> 86.2 us
    pallas_call x1, Pallas kernels: 96 us -> 83.6 us  [local(): pl.pallas_call(kernel, out_shape=shapes, in_specs=[pl.BlockSpec(memory_sp...]
where the time goes in v3:
time: 87 us; the launch traced here: 86.8 us
  Pallas kernels  86.2 us (99%)
    pallas_call x1, Pallas kernels, local(): pl.pallas_call(kernel, out_shape=shapes, in_specs=[pl.BlockSpec(memory_sp...  83.6 us
    pallas_call x1, Pallas kernels, local(): pl.pallas_call(hand_on, out_shape=shapes, in_specs=[pl.BlockSpec(memory_s...  2.59 us

profile of v3, /device:TPU:1, one launch (start us, length us, event | category | flops | bytes accessed | tf_op | source)
XLA Modules:
  0.0 86.8 jit_solution(744333043278898431)
XLA Ops:
  0.6 83.6 %shard_map.85 = (bf16[512,512]{1,0:T(8,128)(2,1)}, bf16[512,1024]{1,0:T(8,128)(2,1)}, bf16[512,512]{1,0:T(8,128)(2,1)}) custom-call(bf16[512,1024]{1,0:T(8,128)(2,1)} %x_hbm.1, bf16[512,128]{1,0:T(8,128)(2,1)} %b_hbm.1, bf16[512,128]{1,0:T(8,128)(2,1)} %c_hbm.1, f32[16,512]{1,0:T(8,128)} %ld_hbm.1, bf16[512,512]{1,0:T(8,128)(2,1)} %sc_hbm.1, ...), custom_call_target="tpu_custom_call" | custom-call | flops 8000000000 | bytes 10000000 | tf_op jit(solution)/shard_map/pallas_call | solution.py:486
  84.3 2.6 %shard_map.86 = (bf16[512,512]{1,0:T(8,128)(2,1)}, bf16[512,1024]{1,0:T(8,128)(2,1)}, bf16[512,512]{1,0:T(8,128)(2,1)}) custom-call(bf16[512,512]{1,0:T(8,128)(2,1)} %get-tuple-element.6.refs_0_, bf16[512,1024]{1,0:T(8,128)(2,1)} %get-tuple-element.7.refs_1_, bf16[512,512]{1,0:T(8,128)(2,1)} %get-tuple-element.8.refs_2_), custom_call_target="tpu_custom_call" | custom-call | bytes 4194304 | tf_op jit(solution)/shard_map/pallas_call | solution.py:497

commit v4 on v3

--- a/solution.py
+++ b/solution.py
@@ -25,8 +25,8 @@
 
 def kernel(
     x_hbm, b_hbm, c_hbm, ld_hbm, sc_hbm, w_hbm,
-    ch_hbm, ig_hbm, sg_hbm,
-    x_ref, b_ref, c_ref, ld_ref, sc_ref, ch_ref, ig_ref, sg_ref, w_v, rise_x, tw_x, bT, cT, cum, g_row, cumT, gT, sco, scoT, mix, mixT, dec,
+    ch_hbm, ig_hbm, own_hbm, left_hbm, right_hbm,
+    x_ref, b_ref, c_ref, ld_ref, sc_ref, ch_ref, ig_ref, w_v, rise_x, tw_x, bT, cT, cum, g_row, cumT, gT, sco, scoT, mix, mixT, dec,
     yl, vl, mid, end, sin, pulled, mixed, gbuf,
     ep_src, ep_dst, tot, rbuf, pbuf, sbuf, sp_src, sp_dst, dt, dtp, dchip, dall,
     pblk, ropp, from_l, from_r,
@@ -66,7 +66,6 @@
     ]
     for copy in loads[:5]:
         copy.start()
-    loads[0].wait()
     pl.semaphore_wait(barrier, 7)
 
     def tell(i, devs):
@@ -77,10 +76,10 @@
         pl.semaphore_wait(round_sem.at[i], 2)
 
     ag = [
-        rcopy(sc_ref.at[LO], gbuf.at[hx, LO], ag_s.at[0], ag_r.at[0], dev_r),
-        rcopy(sc_ref.at[HI], gbuf.at[hx, HI], ag_s.at[1], ag_r.at[1], dev_l),
-        rcopy(sc_ref.at[HI], gbuf.at[hx, HI], ag_s.at[2], ag_r.at[2], dev_r),
-        rcopy(sc_ref.at[LO], gbuf.at[hx, LO], ag_s.at[3], ag_r.at[3], dev_l),
+        rcopy(sc_hbm.at[LO], gbuf.at[hx, LO], ag_s.at[0], ag_r.at[0], dev_r),
+        rcopy(sc_hbm.at[HI], gbuf.at[hx, HI], ag_s.at[1], ag_r.at[1], dev_l),
+        rcopy(sc_hbm.at[HI], gbuf.at[hx, HI], ag_s.at[2], ag_r.at[2], dev_r),
+        rcopy(sc_hbm.at[LO], gbuf.at[hx, LO], ag_s.at[3], ag_r.at[3], dev_l),
         rcopy(gbuf.at[left, LO], gbuf.at[left, LO], ag_s.at[4], ag_r.at[4], dev_r),
         rcopy(gbuf.at[right, HI], gbuf.at[right, HI], ag_s.at[5], ag_r.at[5], dev_l),
     ]
@@ -203,19 +202,18 @@
     core_f = core.astype(F32)
     decay_row = 4 * core + lax.rem(chip, 4)
 
-    def far_first(o):
-        j, k = o // 8, lax.rem(o, 8)
-        dz = 4 + (k // 2) - lax.rem(k, 2) * (k // 2 + (k + 1) // 2)
-        dy = 2 + (j // 2) - lax.rem(j, 2) * (j // 2 + (j + 1) // 2)
-        return 8 * lax.rem(y + dy, 4) + lax.rem(z + dz, 8)
+    at_y = [lax.rem(y + dy, 4) for dy in range(4)]
+    at_z = [lax.rem(z + dz, 8) for dz in range(8)]
+    others = [
+        8 * at_y[dy] + at_z[dz]
+        for dy in (2, 1, 3, 0)
+        for dz in (4, 3, 5, 2, 6, 1, 7, 0)
+        if (dy, dz) != (0, 0)
+    ]
 
     def spread_out(src, dst, ssem, rsem):
-        def body(o, carry):
-            d = far_first(o)
+        for d in others:
             rcopy(src.at[d], dst.at[chip], ssem, rsem, (2 * d + core, hx)).start()
-            return carry
-
-        lax.fori_loop(0, CHIPS - 1, body, 0)
 
     def all_of(src, dst, ssem, rsem):
         part = pl.ds(0, CHIPS - 1)
@@ -242,12 +240,8 @@
                 dec[3:4, 128 * r : 128 * r + 128] = dtp[r : r + 1, :]
             dall[pl.ds(chip, 1)] = dchip[...][None]
 
-            def body(o, carry):
-                d = far_first(o)
+            for d in others:
                 rcopy(dchip, dall.at[chip], d_s.at[1], d_r.at[1], (2 * d + core, hx)).start()
-                return carry
-
-            lax.fori_loop(0, CHIPS - 1, body, 0)
         first = 1.0 - core_f if fwd else core_f
         d_me, d_p = dec[2:3, mine], dec[3:4, mine]
         value = (1.0 - first + first * d_p) * end[k, :, mine] + (
@@ -304,13 +298,15 @@
         pblk[r, slot, at, :] = mm(mixed[at, :], w_v[:, cols]).astype(BF)
 
     def rs_copies(r):
+        into_l = left_hbm if r else from_l
+        into_r = right_hbm if r else from_r
         return [
             rcopy(pblk.at[r, 0, LO], ropp.at[r, 0], rs_s.at[r, 0], rs_r.at[r, 0], dev_r),
             rcopy(pblk.at[r, 0, HI], ropp.at[r, 1], rs_s.at[r, 1], rs_r.at[r, 1], dev_l),
-            rcopy(pblk.at[r, 1, HI], from_l.at[r, HI], rs_s.at[r, 2], rs_r.at[r, 2], dev_r),
-            rcopy(pblk.at[r, 2, LO], from_r.at[r, LO], rs_s.at[r, 3], rs_r.at[r, 3], dev_l),
-            rcopy(pblk.at[r, 1, LO], from_l.at[r, LO], rs_s.at[r, 4], rs_r.at[r, 4], dev_r),
-            rcopy(pblk.at[r, 2, HI], from_r.at[r, HI], rs_s.at[r, 5], rs_r.at[r, 5], dev_l),
+            rcopy(pblk.at[r, 1, HI], into_l.at[HI], rs_s.at[r, 2], rs_r.at[r, 2], dev_r),
+            rcopy(pblk.at[r, 2, LO], into_r.at[LO], rs_s.at[r, 3], rs_r.at[r, 3], dev_l),
+            rcopy(pblk.at[r, 1, LO], into_l.at[LO], rs_s.at[r, 4], rs_r.at[r, 4], dev_r),
+            rcopy(pblk.at[r, 2, HI], into_r.at[HI], rs_s.at[r, 5], rs_r.at[r, 5], dev_l),
         ]
 
     rs = [rs_copies(0), rs_copies(1)]
@@ -342,9 +338,10 @@
     def rs_end(r, out):
         for copy in rs[r][2:]:
             copy.wait_recv()
-        out[...] = (
-            pblk[r, 3].astype(F32) + from_l[r].astype(F32) + from_r[r].astype(F32)
-        ).astype(BF)
+        if out is not None:
+            out[...] = (
+                pblk[r, 3].astype(F32) + from_l[...].astype(F32) + from_r[...].astype(F32)
+            ).astype(BF)
 
     def pull_first():
         def body(n, carry):
@@ -370,7 +367,7 @@
 
     stores = [
         pltpu.make_async_copy(src, dst, out_sem.at[i])
-        for i, (src, dst) in enumerate(((ch_ref, ch_hbm), (ig_ref, ig_hbm), (sg_ref, sg_hbm)))
+        for i, (src, dst) in enumerate(((ch_ref, ch_hbm), (ig_ref, ig_hbm), (pblk.at[1, 3], own_hbm)))
     ]
     loads[4].wait()
     end_state(0, x_ref, tw_x, bT, True, far)
@@ -382,14 +379,15 @@
     heard(2)
     tell(3, (along_y(1), along_y(3)))
     make_table(mixT, cum, gT, scoT)
-    heard(3)
-    ex_out(0, True)
     ag[0].wait_recv()
     ag[4].start()
     ag[1].wait_recv()
     ag[5].start()
+    heard(3)
+    ex_out(0, True)
     ag[2].wait_recv()
     ag[3].wait_recv()
+    loads[0].wait()
     loads[5].wait()
     pull_first()
     ex_back(0, True)
@@ -430,9 +428,9 @@
     finish(2, c_ref, yl, rise_x, mixed, True, far, 2.0)
     rs_first(1)
     rs_second(1)
+    stores[2].start()
     rs_mid(1)
-    rs_end(1, sg_ref)
-    stores[2].start()
+    rs_end(1, None)
     for copy in waits + ag + rs[0] + rs[1]:
         copy.wait_send()
     for copy in stores:
@@ -440,15 +438,25 @@
 
 
 def hand_on(*refs):
-    sources, results, held, in_sem, out_sem = refs[:3], refs[3:6], refs[6:9], refs[9], refs[10]
-    order = (1, 0, 2)
-    loads = [pltpu.make_async_copy(sources[i], held[i], in_sem.at[i]) for i in order]
-    stores = [pltpu.make_async_copy(held[i], results[i], out_sem.at[i]) for i in order]
-    for copy in loads:
-        copy.start()
-    for load, store in zip(loads, stores):
-        load.wait()
-        store.start()
+    sources, results, held, total, in_sem, out_sem = (
+        refs[:5], refs[5:8], refs[8:13], refs[13], refs[14], refs[15]
+    )
+    loads = [pltpu.make_async_copy(sources[i], held[i], in_sem.at[i]) for i in range(5)]
+    stores = [
+        pltpu.make_async_copy(src, results[i], out_sem.at[i])
+        for i, src in enumerate((held[0], held[1], total))
+    ]
+    for i in (2, 3, 4, 1, 0):
+        loads[i].start()
+    for i in (2, 3, 4):
+        loads[i].wait()
+    total[...] = (
+        held[2][...].astype(F32) + held[3][...].astype(F32) + held[4][...].astype(F32)
+    ).astype(BF)
+    stores[2].start()
+    for i in (1, 0):
+        loads[i].wait()
+        stores[i].start()
     for copy in stores:
         copy.wait()
 
@@ -458,7 +466,7 @@
     dma = pltpu.SemaphoreType.DMA
     scratch = [
         vm((512, 1024), BF), vm((512, 128), BF), vm((512, 128), BF), vm((16, 512), F32),
-        vm((512, 512), BF), vm((512, 512), BF), vm((512, 1024), BF), vm((512, 512), BF),
+        vm((512, 512), BF), vm((512, 512), BF), vm((512, 1024), BF),
         vm((1024, 2048), BF), vm((512, 1024), BF), vm((512, 1024), BF),
         vm((128, 512), BF), vm((128, 512), BF),
         vm((16, 512), F32), vm((16, 512), F32), vm((512, 16), F32), vm((512, 16), F32),
@@ -473,7 +481,7 @@
         vm((3, 128, 512), BF), vm((3, 128, 512), BF),
         vm((8, 128), F32), vm((8, 128), F32), vm((8, 128), F32), vm((CHIPS, 8, 128), F32),
         vm((2, 4, 512, 512), BF), vm((2, 2, Q, 512), BF),
-        vm((2, 512, 512), BF), vm((2, 512, 512), BF),
+        vm((512, 512), BF), vm((512, 512), BF),
         dma((6,)), dma((3,)), pltpu.SemaphoreType.REGULAR((4,)), dma((6,)), dma((6,)), dma((3, 4)), dma((3, 4)), dma((2,)), dma((2,)),
         dma((2, 6)), dma((2, 6)),
     ]
@@ -485,9 +493,9 @@
     )
     outs = pl.pallas_call(
         kernel,
-        out_shape=shapes,
+        out_shape=shapes + (shapes[0], shapes[0]),
         in_specs=[pl.BlockSpec(memory_space=pltpu.HBM)] * 6,
-        out_specs=(spec,) * 3,
+        out_specs=(spec,) * 5,
         scratch_shapes=scratch,
         compiler_params=pltpu.CompilerParams(
             collective_id=0, has_side_effects=True, vmem_limit_bytes=58 * 1024 * 1024
@@ -497,10 +505,11 @@
     return pl.pallas_call(
         hand_on,
         out_shape=shapes,
-        in_specs=[pl.BlockSpec(memory_space=pltpu.HBM)] * 3,
+        in_specs=[pl.BlockSpec(memory_space=pltpu.HBM)] * 5,
         out_specs=(spec,) * 3,
-        scratch_shapes=[vm((512, 512), BF), vm((512, 1024), BF), vm((512, 512), BF)]
-        + [dma((3,)), dma((3,))],
+        scratch_shapes=[vm((512, 512), BF), vm((512, 1024), BF)]
+        + [vm((512, 512), BF)] * 4
+        + [dma((5,)), dma((3,))],
         cost_estimate=pl.CostEstimate(flops=0, bytes_accessed=4 * 2**20, transcendentals=0),
     )(*outs)
 

time: 87 us -> 85.4 us (0.982)
  Pallas kernels: 86.2 us -> 84.7 us
    pallas_call x1, Pallas kernels: 83.6 us -> 81.7 us  [local(): pl.pallas_call(kernel, out_shape=shapes + (shapes[0], shapes[0]), in_spec...]
where the time goes in v4:
time: 85.4 us; the launch traced here: 85.3 us
  Pallas kernels  84.7 us (99%)
    pallas_call x1, Pallas kernels, local(): pl.pallas_call(kernel, out_shape=shapes + (shapes[0], shapes[0]), in_spec...  81.7 us
    pallas_call x1, Pallas kernels, local(): pl.pallas_call(hand_on, out_shape=shapes, in_specs=[pl.BlockSpec(memory_s...  2.93 us

profile of v4, /device:TPU:1, one launch (start us, length us, event | category | flops | bytes accessed | tf_op | source)
XLA Modules:
  0.0 85.3 jit_solution(8649144046155535910)
XLA Ops:
  0.6 81.7 %shard_map.85 = (bf16[512,512]{1,0:T(8,128)(2,1)}, bf16[512,1024]{1,0:T(8,128)(2,1)}, bf16[512,512]{1,0:T(8,128)(2,1)}, bf16[512,512]{1,0:T(8,128)(2,1)}, bf16[512,512]{1,0:T(8,128)(2,1)}) custom-call(bf16[512,1024]{1,0:T(8,128)(2,1)} %x_hbm.1, bf16[512,128]{1,0:T(8,128)(2,1)} %b_hbm.1, bf16[512,128]{1,0:T(8,128)(2,1)} %c_hbm.1, f32[16,512]{1,0:T(8,128)} %ld_hbm.1, ...), custom_call_target="tpu_custom_call" | custom-call | flops 8000000000 | bytes 10000000 | tf_op jit(solution)/shard_map/pallas_call | solution.py:494
  82.4 2.9 %shard_map.86 = (bf16[512,512]{1,0:T(8,128)(2,1)}, bf16[512,1024]{1,0:T(8,128)(2,1)}, bf16[512,512]{1,0:T(8,128)(2,1)}) custom-call(bf16[512,512]{1,0:T(8,128)(2,1)} %get-tuple-element.8.refs_0_, bf16[512,1024]{1,0:T(8,128)(2,1)} %get-tuple-element.9.refs_1_, bf16[512,512]{1,0:T(8,128)(2,1)} %get-tuple-element.10.refs_2_, ...), custom_call_target="tpu_custom_call" | custom-call | bytes 4194304 | tf_op jit(solution)/shard_map/pallas_call | solution.py:505
